TPU v7x, 32 devices: a whole 2x2x4 slice. The times are simulated.
32 devices in a mesh: dp: 16 (over z, y, core), tp: 2 (over x).
Axes of the slice: x: 2, y: 2, z: 4, core: 2. Of those that a mesh axis runs over, the one named last changes fastest.
Arguments:
- resid_in: bfloat16 [65536, 1024], P('dp', 'tp'), may hold values from -6 to 6
- norm_gain: bfloat16 [1024], P('tp'), may hold values from 0.5 to 1.5
- proj_gate: bfloat16 [1024, 2048], P('dp', 'tp'), may hold values from -0.1875 to 0.1875
- proj_value: bfloat16 [1024, 2048], P('dp', 'tp'), may hold values from -0.1875 to 0.1875
- proj_state: bfloat16 [1024, 256], P('dp', 'tp'), may hold values from -0.1875 to 0.1875
- proj_step: bfloat16 [1024, 32], P('dp', 'tp'), may hold values from -0.1875 to 0.1875
- conv_value: float32 [4, 2048], P(None, 'tp'), may hold values from -3 to 3
- value_bias: float32 [2048], P('tp'), may hold values from -3 to 3
- conv_state: float32 [4, 256], P(None, 'tp'), may hold values from -3 to 3
- state_bias: float32 [256], P('tp'), may hold values from -3 to 3
- step_bias: float32 [32], P('tp'), may hold values from -4 to 0
- decay_log: float32 [32], P('tp'), may hold values from -5 to 2.5
- skip_gain: float32 [32], P('tp'), may hold values from 0.2 to 1.2
- gate_gain: float32 [2048], P('tp'), may hold values from 0.5 to 1.5
- proj_out: bfloat16 [2048, 1024], P('tp', 'dp'), may hold values from -0.125 to 0.125
- cotangent: bfloat16 [65536, 1024], P('dp', 'tp'), may hold values from -6 to 6
Outputs:
- block_out: bfloat16 [65536, 1024], P('dp', 'tp')
- grad_in: bfloat16 [65536, 1024], P('dp', 'tp')
- grad_norm_gain: float32 [1024], P('tp')
- grad_proj_gate: float32 [1024, 2048], P('dp', 'tp')
- grad_proj_value: float32 [1024, 2048], P('dp', 'tp')
- grad_proj_state: float32 [1024, 256], P('dp', 'tp')
- grad_proj_step: float32 [1024, 32], P('dp', 'tp')
- grad_conv_value: float32 [4, 2048], P(None, 'tp')
- grad_value_bias: float32 [2048], P('tp')
- grad_conv_state: float32 [4, 256], P(None, 'tp')
- grad_state_bias: float32 [256], P('tp')
- grad_step_bias: float32 [32], P('tp')
- grad_decay_log: float32 [32], P('tp')
- grad_skip_gain: float32 [32], P('tp')
- grad_gate_gain: float32 [2048], P('tp')
- grad_proj_out: float32 [2048, 1024], P('tp', 'dp')
All inputs are finite; a program needn't handle non-finite values.
Results may differ from a plain program's by a relative error of at most 0.012.
The roundings to bfloat16 on the way count: a program that leaves them out, or rounds other values in their place, can miss the bound.
Values may be sent and summed in bfloat16 or wider, within the bound.
A program may use at most 384 MiB of HBM per device.

v0:
```python
from functools import partial

import jax
import jax.numpy as jnp
from jax import lax
from jax.sharding import PartitionSpec as P

D = 1024
HEADDIM = 64
GROUP = 256
SEQ = 2048
INNER = 2048


epsilon = 1e-05


def causal_conv(signal, kernel, kernel_bias):
    kernel_len = kernel.shape[0]
    length = signal.shape[0]
    padded = jnp.pad(signal, ((kernel_len - 1, 0), (0, 0)))
    summed = jnp.broadcast_to(kernel_bias[None, :], signal.shape)
    for offset in range(kernel_len):
        summed = summed + kernel[offset][None, :] * padded[offset : offset + length]
    return summed


def group_step(decay_rate, skip_gain, carried, pieces):
    highest = lax.Precision.HIGHEST
    values, step_size, enter_map, read_map = pieces
    block_len = values.shape[0]
    log_decay = jnp.cumsum(step_size * decay_rate[None, :], axis=0)
    lower_mask = jnp.tril(jnp.ones((block_len, block_len), dtype=bool))
    decay_diff = log_decay[:, None, :] - log_decay[None, :, :]
    decay_mask = jnp.exp(jnp.where(lower_mask[:, :, None], decay_diff, -jnp.inf))
    scores = jnp.dot(read_map, enter_map.T, precision=highest)
    weights = scores[:, :, None] * decay_mask * step_size[None, :, :]
    within = jnp.einsum("ijh,jhp->ihp", weights, values, precision=highest)
    across = (
        jnp.einsum("is,hps->ihp", read_map, carried, precision=highest)
        * jnp.exp(log_decay)[:, :, None]
    )
    to_end = jnp.exp(log_decay[-1][None, :] - log_decay) * step_size
    scaled_values = values * to_end[:, :, None]
    updated = jnp.exp(log_decay[-1])[:, None, None] * carried + jnp.einsum(
        "jhp,js->hps", scaled_values, enter_map, precision=highest
    )
    result = within + across + skip_gain[None, :, None] * values
    return (updated, result)


def ssd(values, step_size, enter_map, read_map, decay_rate, skip_gain, group_len):
    total_len, head_count, head_dim = values.shape
    state_dim = enter_map.shape[1]
    blocks = total_len // group_len
    pieces = (
        values.reshape(blocks, group_len, head_count, head_dim),
        step_size.reshape(blocks, group_len, head_count),
        enter_map.reshape(blocks, group_len, state_dim),
        read_map.reshape(blocks, group_len, state_dim),
    )
    start = jnp.zeros((head_count, head_dim, state_dim), values.dtype)
    stepper = jax.checkpoint(partial(group_step, decay_rate, skip_gain))
    finals, outputs = lax.scan(stepper, start, pieces)
    return outputs.reshape(total_len, head_count, head_dim)


def product(matrix, factor):
    return jnp.dot(matrix, factor, preferred_element_type=jnp.float32)


def product_left(matrix, factor):
    return jnp.einsum("tk,tc->kc", matrix, factor, preferred_element_type=jnp.float32)


def product_right(matrix, factor):
    return jnp.einsum("tc,kc->tk", matrix, factor, preferred_element_type=jnp.float32)


def gating(mixed_in, gate_in):
    return mixed_in * jax.nn.silu(gate_in)


def local(
    resid_in,
    norm_gain,
    proj_gate,
    proj_value,
    proj_state,
    proj_step,
    conv_value,
    value_bias,
    conv_state,
    state_bias,
    step_bias,
    decay_log,
    skip_gain,
    gate_gain,
    proj_out,
    cotangent,
):
    resid_full, gain_row, cot_full = (
        lax.all_gather(resid_in, "tp", axis=1, tiled=True),
        lax.all_gather(norm_gain[None, :], "tp", axis=1, tiled=True),
        lax.all_gather(cotangent, "tp", axis=1, tiled=True),
    )
    gate_w, value_w, state_w, step_w, out_w = (
        lax.all_gather(proj_gate, "dp", axis=0, tiled=True),
        lax.all_gather(proj_value, "dp", axis=0, tiled=True),
        lax.all_gather(proj_state, "dp", axis=0, tiled=True),
        lax.all_gather(proj_step, "dp", axis=0, tiled=True),
        lax.all_gather(proj_out, "dp", axis=1, tiled=True),
    )
    resid_wide = resid_full.astype(jnp.float32)
    inv_rms = lax.rsqrt(jnp.mean(resid_wide * resid_wide, axis=-1, keepdims=True) + epsilon)
    unit_rows = resid_wide * inv_rms
    gain_wide = gain_row.astype(jnp.float32)
    normed_in = (unit_rows * gain_wide).astype(jnp.bfloat16)
    gate_raw = product(normed_in, gate_w)
    value_raw = product(normed_in, value_w)
    state_raw = product(normed_in, state_w)
    step_raw = product(normed_in, step_w)
    seq_count = resid_in.shape[0] // SEQ

    def conv_act(raw, kernel, kernel_bias):
        framed = raw.reshape(seq_count, SEQ, raw.shape[1])
        convolved = jax.vmap(causal_conv, (0, None, None))(framed, kernel, kernel_bias)
        return jax.nn.silu(convolved).reshape(raw.shape)

    value_act, value_pull = jax.vjp(conv_act, value_raw, conv_value, value_bias)
    values = value_act.astype(jnp.bfloat16)
    state_act, state_pull = jax.vjp(conv_act, state_raw, conv_state, state_bias)
    maps = lax.all_gather(state_act.astype(jnp.bfloat16), "tp", axis=1, tiled=True)
    head_count = step_raw.shape[1]
    state_dim = maps.shape[1] // 2

    def mixer(values_in, maps_in, step_in, bias_in, log_in, skip_in):
        step_size = jax.nn.softplus(step_in + bias_in)
        scan_one = partial(ssd, group_len=GROUP)
        mixed_out = jax.vmap(scan_one, (0, 0, 0, 0, None, None))(
            values_in.reshape(seq_count, SEQ, head_count, HEADDIM),
            step_size.reshape(seq_count, SEQ, head_count),
            maps_in[:, :state_dim].reshape(seq_count, SEQ, state_dim),
            maps_in[:, state_dim:].reshape(seq_count, SEQ, state_dim),
            -jnp.exp(log_in),
            skip_in,
        )
        return mixed_out.reshape(values_in.shape)

    mixed, mixer_pull = jax.vjp(
        mixer,
        values.astype(jnp.float32),
        maps.astype(jnp.float32),
        step_raw,
        step_bias,
        decay_log,
        skip_gain,
    )
    gated, gate_pull = jax.vjp(gating, mixed, gate_raw)
    squares = lax.psum(jnp.sum(gated * gated, axis=-1), "tp")
    gate_scale = lax.rsqrt(squares / INNER + epsilon)[:, None]
    scaled = gated * gate_scale
    normed_out = (scaled * gate_gain).astype(jnp.bfloat16)
    out_terms = product(normed_out, out_w)
    out_mine = lax.psum_scatter(out_terms, "tp", scatter_dimension=1, tiled=True)
    block_out = (resid_in.astype(jnp.float32) + out_mine).astype(jnp.bfloat16)
    normed_grad = product_right(cot_full, out_w)
    out_grad = product_left(normed_out, cot_full)
    gate_gain_grad = jnp.sum(normed_grad * scaled, axis=0)
    weighted = normed_grad * gate_gain
    crossed = lax.psum(jnp.sum(weighted * gated, axis=-1), "tp")
    cubed = gate_scale * gate_scale * gate_scale
    gated_grad = weighted * gate_scale - gated * cubed * (crossed[:, None] / INNER)
    mixed_grad, gate_raw_grad = gate_pull(gated_grad)
    values_grad, maps_grad, step_grad, step_bias_grad, decay_grad, skip_grad = mixer_pull(
        mixed_grad
    )
    maps_mine = lax.psum_scatter(maps_grad, "tp", scatter_dimension=1, tiled=True)
    value_raw_grad, conv_value_grad, value_bias_grad = value_pull(values_grad)
    state_raw_grad, conv_state_grad, state_bias_grad = state_pull(maps_mine)
    gate_low = gate_raw_grad.astype(jnp.bfloat16)
    value_low = value_raw_grad.astype(jnp.bfloat16)
    state_low = state_raw_grad.astype(jnp.bfloat16)
    step_low = step_grad.astype(jnp.bfloat16)
    gate_w_grad = product_left(normed_in, gate_low)
    value_w_grad = product_left(normed_in, value_low)
    state_w_grad = product_left(normed_in, state_low)
    step_w_grad = product_left(normed_in, step_low)
    input_terms = (
        product_right(gate_low, gate_w)
        + product_right(value_low, value_w)
        + product_right(state_low, state_w)
        + product_right(step_low, step_w)
    )
    width_mine = resid_in.shape[1]
    start = lax.axis_index("tp") * width_mine
    unit_mine = lax.dynamic_slice_in_dim(unit_rows, start, width_mine, 1)
    resid_mine = resid_in.astype(jnp.float32)
    gain_mine = norm_gain.astype(jnp.float32)
    input_whole = lax.psum(input_terms, "tp")
    crossed_rows = jnp.sum(input_whole * gain_wide * resid_wide, axis=-1)
    input_mine = lax.dynamic_slice_in_dim(input_whole, start, width_mine, 1)
    pulled = input_mine * gain_mine
    rms_cubed = inv_rms * inv_rms * inv_rms
    grad_in = (
        cotangent.astype(jnp.float32)
        + pulled * inv_rms
        - resid_mine * rms_cubed * (crossed_rows[:, None] / D)
    ).astype(jnp.bfloat16)
    gain_grad = jnp.sum(input_mine * unit_mine, axis=0)
    large_sums = (
        lax.psum_scatter(gate_w_grad, "dp", scatter_dimension=0, tiled=True),
        lax.psum_scatter(value_w_grad, "dp", scatter_dimension=0, tiled=True),
        lax.psum_scatter(state_w_grad, "dp", scatter_dimension=0, tiled=True),
        lax.psum_scatter(step_w_grad, "dp", scatter_dimension=0, tiled=True),
        lax.psum_scatter(out_grad, "dp", scatter_dimension=1, tiled=True),
    )
    small_sums = lax.psum(
        (
            gain_grad,
            conv_value_grad,
            value_bias_grad,
            conv_state_grad,
            state_bias_grad,
            step_bias_grad,
            decay_grad,
            skip_grad,
            gate_gain_grad,
        ),
        "dp",
    )
    return (
        block_out,
        grad_in,
        small_sums[0],
        large_sums[0],
        large_sums[1],
        large_sums[2],
        large_sums[3],
        small_sums[1],
        small_sums[2],
        small_sums[3],
        small_sums[4],
        small_sums[5],
        small_sums[6],
        small_sums[7],
        small_sums[8],
        large_sums[4],
    )


def solution(mesh):
    return jax.shard_map(
        local,
        mesh=mesh,
        in_specs=(
            P("dp", "tp"),
            P("tp"),
            P("dp", "tp"),
            P("dp", "tp"),
            P("dp", "tp"),
            P("dp", "tp"),
            P(None, "tp"),
            P("tp"),
            P(None, "tp"),
            P("tp"),
            P("tp"),
            P("tp"),
            P("tp"),
            P("tp"),
            P("tp", "dp"),
            P("dp", "tp"),
        ),
        out_specs=(
            P("dp", "tp"),
            P("dp", "tp"),
            P("tp"),
            P("dp", "tp"),
            P("dp", "tp"),
            P("dp", "tp"),
            P("dp", "tp"),
            P(None, "tp"),
            P("tp"),
            P(None, "tp"),
            P("tp"),
            P("tp"),
            P("tp"),
            P("tp"),
            P("tp"),
            P("tp", "dp"),
        ),
        check_vma=False,
    )
```

profile of v0, /device:TPU:0, one launch (start us, length us, event | category | flops | bytes accessed | tf_op | source)
XLA Modules:
  0.0 2525.6 jit_solution(9766520769599865508)
XLA Ops:
  15.5 23.2 all_gather.31
  38.6 77.6 %all-gather.10.cloned.1.call-done = bf16[4096,1024]{1,0:T(8,128)(2,1)} async-done(((bf16[4096,512]{1,0:T(8,128)(2,1)}), bf16[4096,1024]{1,0:T(8,128)(2,1)}) %all-gather.10.cloned.1.call-update) | async-done | bytes 8388624 | tf_op jit(solution)/shard_map/all_gather | solution.py:103
  139.2 21.8 all-gather.2
  161.7 16.1 fusion.132
  177.7 17.4 copy.203
  195.2 33.4 %fusion.107 = (f32[2,2048,1024]{1,2,0:T(8,128)}, f32[2,2048,1024]{1,2,0:T(8,128)}) fusion(f32[2,2048,1024]{1,2,0:T(8,128)} %copy.203, f32[1024]{0:T(1024)S(1)} %bitcast.447, f32[1024]{0:T(1024)S(1)} %bitcast.449, f32[1024]{0:T(1024)S(1)} %bitcast.445, f32[1024]{0:T(1024)S(1)} %bitcast.443, f32[1024]{0:T(1024)S(1)} %copy-done.54), kind=kLoop, calls=%fused_computation.174 | loop fusion | flops 58720256 | bytes 50352128 | tf_op jit(solution)/shard_map/jvp(vmap())/transpose | solution.py:64
  269.8 201.1 %while.43 = (s32[]{:T(128)}, f32[2,16,64,128]{3,2,1,0:T(8,128)S(1)}, f32[8,2,256,16,64]{2,4,3,1,0:T(8,128)}, f32[8,2,16,64,128]{4,3,2,1,0:T(8,128)}, f32[8,2,256...) while((s32[]{:T(128)}, ...), condition=%wide.region_4.5_spmd.clone, body=%wide.region_1.4_spmd.clone.sunk | while | flops 3435954176 | bytes 20586076 | solution.py:64
  470.9 17.7 copy.209
  488.6 18.2 reshape.340
  506.8 26.3 %multiply_reduce_fusion.11 = (f32[4096]{0:T(1024)S(1)}, f32[4096,1024]{0,1:T(8,128)}, f32[4096,1024]{0,1:T(8,128)}) fusion(f32[4096,1024]{0,1:T(8,128)} %reshape.340, bf16[4096,1024]{1,0:T(8,128)(2,1)} %copy-done.1, bf16[1024,1024]{1,0:T(8,128)(2,1)} %all-gather.16.cloned.1.call-done), kind=kOutput, calls=%fused_computation.158 | convolution fusion | flops 8619290624 | bytes 60833792 | tf_op jit(solution)/shard_map/dot_general | solution.py:69
  540.2 20.7 multiply_reduce_fusion.5
  569.2 32.4 %fusion.98 = (bf16[4096,1024]{0,1:T(8,128)(2,1)}, f32[4096,1024]{0,1:T(8,128)}) fusion(f32[4096,1024]{0,1:T(8,128)} %get-tuple-element.822, f32[4096,1024]{0,1:T(8,128)} %reshape.340, f32[4096]{0:T(1024)S(1)} %broadcast_multiply_fusion.9, f32[4096,1024]{0,1:T(8,128)} %get-tuple-element.770, f32[4096]{0:T(1024)S(1)} %get-tuple-element.808, ...), kind=kLoop, calls=%fused_computation.141 | loop fusion | flops 75497472 | bytes 92327936 | tf_op jit(solution)/shard_map/convert_element_type | solution.py:181
  637.3 798.8 %while.44 = (s32[]{:T(128)}, f32[16]{0:T(128)}, f32[16]{0:T(128)}, f32[2,16,64,128]{3,2,1,0:T(8,128)}, f32[8,2,256,16,64]{2,4,3,1,0:T(8,128)}, /*index=5*/f32[8,...) while((s32[]{:T(128)}, f32[16]{0:T(128)}, f32[16]{0:T(128)}, ...), condition=%wide.region_25.26_spmd.clone, body=%wide.region_10.25_spmd.clone.sunk | while | flops 7897800704 | bytes 68460440 | solution.py:64
  1440.7 19.3 copy.215
  1460.0 18.1 reshape.342
  1478.1 41.3 %multiply_reduce_fusion.9 = (f32[1024]{0:T(1024)}, f32[1024]{0:T(1024)}, f32[1024]{0:T(1024)}, f32[1024]{0:T(1024)}, f32[1024]{0:T(1024)}, /*index=5*/f32[2,2048,1024]{1,2,0:T(8,128)}) fusion(f32[2,2048,1024]{1,2,0:T(8,128)} %copy.203, f32[2,2048,1024]{1,2,0:T(8,128)} %get-tuple-element.774, f32[2,2048,1024]{1,2,0:T(8,128)} %reshape.342), kind=kLoop, calls=%fused_computation.153 | loop fusion | flops 75492352 | bytes 67129344 | tf_op jit(solution)/shard_map/transpose(jvp(vmap()))/reduce_sum | solution.py:24
  1519.4 28.4 %broadcast_multiply_fusion.1 = (f32[2,2048,1024]{1,2,0:T(8,128)}, f32[2,2048,1024]{1,2,0:T(8,128)}, f32[2,2048,1024]{1,2,0:T(8,128)}, f32[2,2048,1024]{1,2,0:T(8,128)}) fusion(f32[2,2048,1024]{1,2,0:T(8,128)} %get-tuple-element.768, f32[1024]{0:T(1024)S(1)} %bitcast.448, f32[1024]{0:T(1024)S(1)} %bitcast.444, f32[1024]{0:T(1024)S(1)} %bitcast.446, ...), kind=kLoop, calls=%fused_computation.177 | loop fusion | flops 16777216 | bytes 83902464 | tf_op jit(solution)/shard_map/transpose(jvp(vmap()))/mul | solution.py:24
  1547.8 27.4 %fusion.101 = bf16[2,2048,1024]{1,2,0:T(8,128)(2,1)} fusion(f32[2,2048,1024]{1,2,0:T(8,128)} %get-tuple-element.794, f32[2,2048,1024]{1,2,0:T(8,128)} %get-tuple-element.795, f32[2,2048,1024]{1,2,0:T(8,128)} %get-tuple-element.796, f32[2,2048,1024]{1,2,0:T(8,128)} %get-tuple-element.793), kind=kLoop, calls=%fused_computation.145 | loop fusion | flops 16777216 | bytes 75497472 | tf_op jit(solution)/shard_map/convert.4
  1604.8 15.2 fusion.135
  1620.0 14.7 fusion.134
  1639.4 23.3 add_add_fusion
  1664.4 17.4 fusion.122
  1681.9 15.1 fusion.137
  1697.0 16.9 fusion.121
  1714.1 15.3 fusion.136
  1738.3 299.8 %all-reduce.25.cloned.1.call-done = f32[4096,1024]{1,0:T(8,128)} async-done(((f32[4096,1024]{1,0:T(8,128)}), f32[4096,1024]{1,0:T(8,128)}) %all-reduce.25.cloned.1.call-update) | async-done | bytes 16777232 | tf_op jit(solution)/shard_map/psum | solution.py:200
  2047.3 182.5 %reduce-scatter.10.cloned.1.call-done = f32[4096,512]{1,0:T(8,128)} async-done(((f32[4096,1024]{1,0:T(8,128)}), f32[4096,512]{1,0:T(8,128)}) %reduce-scatter.10.cloned.1.call-update) | async-done | bytes 8388624 | tf_op jit(solution)/shard_map/reduce_scatter | solution.py:165
  2229.9 16.0 multiply_reduce_fusion.12
  2245.9 62.7 %all-reduce.22 = (f32[512]{0:T(512)}, f32[4,1024]{1,0:T(4,128)}, f32[1024]{0:T(1024)}, f32[4,128]{1,0:T(4,128)}, f32[128]{0:T(128)}, /*index=5*/f32[16]{0:T(128)}, f32[16]{0:T(128)}, f32[16]{0:T(128)}, f32[1024]{0:T(1024)}) all-reduce(f32[512]{0:T(512)S(1)} %get-tuple-element.791, ...), channel_id=1, replica_groups=mesh['dp'=16,'tp'=2] {'dp'}, use_global_device_ids=true, to_apply=%region_30.31 | all-reduce | flops 7344 | bytes 58752 | tf_op jit(solution)/shard_map/psum | solution.py:218
  2308.6 75.1 %reduce-scatter.20.cloned.1.call-done = f32[1024,64]{0,1:T(8,128)} async-done(((f32[1024,1024]{0,1:T(8,128)}), f32[1024,64]{0,1:T(8,128)}) %reduce-scatter.20.cloned.1.call-update) | async-done | bytes 262160 | tf_op jit(solution)/shard_map/reduce_scatter | solution.py:216
  2383.7 75.8 %reduce-scatter.14.cloned.1.call-done = f32[64,1024]{1,0:T(8,128)} async-done(((f32[1024,1024]{1,0:T(8,128)}), f32[64,1024]{1,0:T(8,128)}) %reduce-scatter.14.cloned.1.call-update) | async-done | bytes 262160 | tf_op jit(solution)/shard_map/reduce_scatter | solution.py:212
  2459.5 59.3 %reduce-scatter.18.cloned.1.call-done = f32[64,128]{1,0:T(8,128)} async-done(((f32[1024,128]{1,0:T(8,128)}), f32[64,128]{1,0:T(8,128)}) %reduce-scatter.18.cloned.1.call-update) | async-done | bytes 32784 | tf_op jit(solution)/shard_map/reduce_scatter | solution.py:214
  (916 shorter events, 1154.9 us)
Async XLA Ops:
  7.2 109.1 %all-gather.10.cloned.1.call-start = ((), (), s32[]{:S(2)}) async-start(), calls=%async_computation.7 | async-start | bytes 12582912 | tf_op jit(solution)/shard_map/all_gather | solution.py:103
  7.9 153.8 %all-gather.12.cloned.1.call-start = ((), (), s32[]{:S(2)}) async-start(), calls=%async_computation.8 | async-start | bytes 2228224 | tf_op jit(solution)/shard_map/all_gather | solution.py:109
  8.7 248.6 %all-gather.14.cloned.1.call-start = ((), (), s32[]{:S(2)}) async-start(), calls=%async_computation.9 | async-start | bytes 3145728 | tf_op jit(solution)/shard_map/all_gather | solution.py:133
  9.5 124.6 %copy-start.46 = (f32[128]{0:T(128)}, f32[128]{0:T(128)S(1)}, u32[]{:S(2)}) copy-start(f32[128]{0:T(128)S(1)} %get-tuple-element.814) | copy-start | bytes 1540
  9.5 124.6 %copy-start.48 = (f32[128]{0:T(128)}, f32[128]{0:T(128)S(1)}, u32[]{:S(2)}) copy-start(f32[128]{0:T(128)S(1)} %get-tuple-element.815) | copy-start | bytes 1540
  9.6 124.6 %copy-start.50 = (f32[128]{0:T(128)}, f32[128]{0:T(128)S(1)}, u32[]{:S(2)}) copy-start(f32[128]{0:T(128)S(1)} %get-tuple-element.816) | copy-start | bytes 1540
  9.6 124.6 %copy-start.52 = (f32[128]{0:T(128)}, f32[128]{0:T(128)S(1)}, u32[]{:S(2)}) copy-start(f32[128]{0:T(128)S(1)} %get-tuple-element.817) | copy-start | bytes 1540
  15.5 113.0 %copy-start.23 = (f32[2,1,512]{2,1,0:T(1,128)}, f32[2,1,512]{2,1,0:T(1,128)S(1)}, u32[]{:S(2)}) copy-start(f32[2,1,512]{2,1,0:T(1,128)S(1)} %mul.891) | copy-start | bytes 12292
  38.6 89.9 %copy-start.11 = (bf16[1024,128]{1,0:T(8,128)(2,1)}, bf16[1024,128]{1,0:T(8,128)(2,1)S(1)}, u32[]{:S(2)}) copy-start(bf16[1024,128]{1,0:T(8,128)(2,1)S(1)} %all_gather.31) | copy-start | bytes 786436
  137.2 369.6 %all-gather.16.cloned.1.call-start = ((), (), s32[]{:S(2)}) async-start(), calls=%async_computation.10 | async-start | bytes 2228224 | tf_op jit(solution)/shard_map/all_gather | solution.py:108
  137.8 402.4 %all-gather.18.cloned.1.call-start = ((), (), s32[]{:S(2)}) async-start(), calls=%async_computation.11 | async-start | bytes 2228224 | tf_op jit(solution)/shard_map/all_gather | solution.py:112
  138.4 401.8 %all-gather.20.cloned.1.call-start = ((), (), s32[]{:S(2)}) async-start(), calls=%async_computation.13 | async-start | bytes 12582912 | tf_op jit(solution)/shard_map/all_gather | solution.py:105
  138.9 1495.8 %reduce-scatter.12.cloned.1.call-start = ((), (), s32[]{:S(2)}) async-start(), calls=%async_computation.14 | async-start | bytes 6291456 | tf_op jit(solution)/shard_map/reduce_scatter | solution.py:178
  139.1 56.1 %copy-start.25 = (f32[1,1024]{1,0:T(1,128)}, f32[1,1024]{1,0:T(1,128)S(1)}, u32[]{:S(2)}) copy-start(f32[1,1024]{1,0:T(1,128)S(1)} %get-tuple-element.810) | copy-start | bytes 12292
  139.1 56.1 %copy-start.27 = (f32[1,1024]{1,0:T(1,128)}, f32[1,1024]{1,0:T(1,128)S(1)}, u32[]{:S(2)}) copy-start(f32[1,1024]{1,0:T(1,128)S(1)} %get-tuple-element.811) | copy-start | bytes 12292
  139.1 56.1 %copy-start.29 = (f32[1,1024]{1,0:T(1,128)}, f32[1,1024]{1,0:T(1,128)S(1)}, u32[]{:S(2)}) copy-start(f32[1,1024]{1,0:T(1,128)S(1)} %get-tuple-element.812) | copy-start | bytes 12292
  139.1 56.1 %copy-start.31 = (f32[1,1024]{1,0:T(1,128)}, f32[1,1024]{1,0:T(1,128)S(1)}, u32[]{:S(2)}) copy-start(f32[1,1024]{1,0:T(1,128)S(1)} %get-tuple-element.813) | copy-start | bytes 12292
  161.1 89.9 %copy-start.15 = (bf16[1024,16]{0,1:T(8,128)(2,1)}, bf16[1024,16]{0,1:T(8,128)(2,1)S(1)}, u32[]{:S(2)}) copy-start(bf16[1024,16]{0,1:T(8,128)(2,1)S(1)} %reshape.355) | copy-start | bytes 98308
  1440.7 289.1 %reduce-scatter.22.cloned.1.call-start = ((), (), s32[]{:S(2)}) async-start(), calls=%async_computation.20 | async-start | bytes 557056
  1478.1 41.3 %copy-start.26 = (f32[1,1024]{1,0:T(1,128)S(1)}, f32[1,1024]{1,0:T(1,128)}, u32[]{:S(2)}) copy-start(f32[1,1024]{1,0:T(1,128)} %copy-done.25) | copy-start | bytes 12292
  1478.1 41.3 %copy-start.28 = (f32[1,1024]{1,0:T(1,128)S(1)}, f32[1,1024]{1,0:T(1,128)}, u32[]{:S(2)}) copy-start(f32[1,1024]{1,0:T(1,128)} %copy-done.27) | copy-start | bytes 12292
  1478.1 41.3 %copy-start.30 = (f32[1,1024]{1,0:T(1,128)S(1)}, f32[1,1024]{1,0:T(1,128)}, u32[]{:S(2)}) copy-start(f32[1,1024]{1,0:T(1,128)} %copy-done.29) | copy-start | bytes 12292
  1478.1 41.3 %copy-start.32 = (f32[1,1024]{1,0:T(1,128)S(1)}, f32[1,1024]{1,0:T(1,128)}, u32[]{:S(2)}) copy-start(f32[1,1024]{1,0:T(1,128)} %copy-done.31) | copy-start | bytes 12292
  1604.7 433.4 %all-reduce.25.cloned.1.call-start = ((), (), s32[]{:S(2)}) async-start(), calls=%async_computation.15 | async-start | bytes 33554432 | tf_op jit(solution)/shard_map/psum | solution.py:200
  1662.8 567.0 %reduce-scatter.10.cloned.1.call-start = ((), (), s32[]{:S(2)}) async-start(), calls=%async_computation.12 | async-start | bytes 25165824 | tf_op jit(solution)/shard_map/reduce_scatter | solution.py:165
  1681.8 626.8 %reduce-scatter.16.cloned.1.call-start = ((), (), s32[]{:S(2)}) async-start(), calls=%async_computation.17 | async-start | bytes 4456448 | tf_op jit(solution)/shard_map/reduce_scatter | solution.py:213
  1697.0 686.7 %reduce-scatter.20.cloned.1.call-start = ((), (), s32[]{:S(2)}) async-start(), calls=%async_computation.19 | async-start | bytes 4456448 | tf_op jit(solution)/shard_map/reduce_scatter | solution.py:216
  1714.0 745.5 %reduce-scatter.14.cloned.1.call-start = ((), (), s32[]{:S(2)}) async-start(), calls=%async_computation.16 | async-start | bytes 4456448 | tf_op jit(solution)/shard_map/reduce_scatter | solution.py:212
  1729.3 308.8 %copy-start.24 = (f32[2,1,512]{2,1,0:T(1,128)S(1)}, f32[2,1,512]{2,1,0:T(1,128)}, u32[]{:S(2)}) copy-start(f32[2,1,512]{2,1,0:T(1,128)} %copy-done.23) | copy-start | bytes 12292
  1729.4 789.4 %reduce-scatter.18.cloned.1.call-start = ((), (), s32[]{:S(2)}) async-start(), calls=%async_computation.18 | async-start | bytes 557056 | tf_op jit(solution)/shard_map/reduce_scatter | solution.py:214
  1738.3 491.6 %copy-start.18 = (f32[4096]{0:T(1024)S(1)}, f32[4096]{0:T(1024)}, u32[]{:S(2)}) copy-start(f32[4096]{0:T(1024)} %copy-done.17) | copy-start | bytes 49156
  1738.3 491.6 %copy-start.19 = (f32[4096]{0:T(1024)S(1)}, f32[4096]{0:T(1024)}, u32[]{:S(2)}) copy-start(f32[4096]{0:T(1024)} %get-tuple-element.806) | copy-start | bytes 49156
  (121 other events, 1459.7 us)
Sparse Core Ops, SparseCore 0:
  9.6 106.6 all-gather.9
  118.5 41.5 all-gather.11
  162.2 31.9 all-gather.13
  196.2 41.3 all-gather.15
  239.7 40.1 all-gather.17
  281.2 102.8 all-gather.19
  1440.8 51.4 reduce-scatter.11
  1604.9 53.0 reduce-scatter.21
  1662.9 375.1 all-reduce.24
  2040.3 189.4 reduce-scatter.9
  2234.3 73.0 reduce-scatter.15
  2312.1 71.5 reduce-scatter.19
  2388.1 71.3 reduce-scatter.13
  2463.9 54.8 reduce-scatter.17
where the time goes:
time: 2540 us; the launch traced here: 2530 us
  matrix products  800 us (31%)
  waiting for transfers between devices  773 us (30%)
  local copies, waits for them, and re-layouts  396 us (16%)
  other arithmetic  385 us (15%)
  blocking collectives  128 us (5%)
  loops' own time  27.3 us (1%)
    psum x1, waiting for transfers between devices, local(): input_whole = lax.psum(input_terms, 'tp')  300 us
    dot_general x24, matrix products, group_step(): within = jnp.einsum('ijh,jhp->ihp', weights, values, precision=highest)  284 us
    reduce_scatter x1, waiting for transfers between devices, local(): lax.psum_scatter(out_terms, 'tp', scatter_dimension=1, tiled=True)  183 us
    dot_general x32, matrix products, group_step(): jnp.einsum('is,hps->ihp', read_map, carried, precision=highest)  129 us
    dot_general x24, matrix products, group_step(): jnp.einsum('jhp,js->hps', scaled_values, enter_map, precision=highest)  111 us
    another operation x74, other arithmetic  88.9 us
    dot_general x5, matrix products, product_right(): jnp.einsum('tc,kc->tk', matrix, factor, preferred_element_type=jnp.float32)  82.1 us
    all_gather x1, waiting for transfers between devices, local(): lax.all_gather(resid_in, 'tp', axis=1, tiled=True)  77.6 us
  transfers between devices with their start and end apart: 14, of which 6 were waited for; matrix products, arithmetic and copies ran while one was open for 28% of the time, Pallas kernels for 0%

commit v1 on v0

--- a/solution.py
+++ b/solution.py
@@ -3,6 +3,8 @@
 import jax
 import jax.numpy as jnp
 from jax import lax
+from jax.experimental import pallas as pl
+from jax.experimental.pallas import tpu as pltpu
 from jax.sharding import PartitionSpec as P
 
 D = 1024
@@ -81,7 +83,7 @@
     return mixed_in * jax.nn.silu(gate_in)
 
 
-def local(
+def by_heads(
     resid_in,
     norm_gain,
     proj_gate,
@@ -249,7 +251,438 @@
     )
 
 
+CHUNK = 128
+QUAD = 8
+WIDE = QUAD * HEADDIM
+F32 = jnp.float32
+BF16 = jnp.bfloat16
+
+
+def nt(left, right):
+    return lax.dot_general(left, right, (((1,), (1,)), ((), ())), preferred_element_type=F32)
+
+
+def nn(left, right):
+    return jnp.dot(left, right, preferred_element_type=F32)
+
+
+def parts(v):
+    high = v.astype(BF16)
+    return high, (v - high.astype(F32)).astype(BF16)
+
+
+def twice(v, axis=1):
+    return jnp.concatenate([v, v], axis=axis)
+
+
+def stacked(pair, axis=0):
+    return jnp.concatenate(pair, axis=axis)
+
+
+def nt_parts(left, right):
+    return nt(left[0], right[0]) + nt(left[0], right[1]) + nt(left[1], right[0])
+
+
+def pair_columns(ref, pair, lane_low):
+    first = jnp.broadcast_to(ref[0, :, 2 * pair : 2 * pair + 1], (CHUNK, 128))
+    second = jnp.broadcast_to(ref[0, :, 2 * pair + 1 : 2 * pair + 2], (CHUNK, 128))
+    return first, second, jnp.where(lane_low, first, second)
+
+
+def two_heads(block, lane_low):
+    zero = jnp.zeros_like(block)
+    return jnp.concatenate([jnp.where(lane_low, block, zero), jnp.where(lane_low, zero, block)], axis=0)
+
+
+def scan_forward(per_seq, x_ref, b_ref, c_ref, bt_ref, acol_ref, dtcol_ref, arow_ref, skip_ref, y_ref, st_ref, state, scores):
+    step, quad = pl.program_id(0), pl.program_id(1)
+    row = lax.broadcasted_iota(jnp.int32, (CHUNK, CHUNK), 0)
+    col = lax.broadcasted_iota(jnp.int32, (CHUNK, CHUNK), 1)
+    lane_low = col < HEADDIM
+
+    @pl.when(lax.rem(step, per_seq) == 0)
+    def _():
+        state[quad] = jnp.zeros((CHUNK, WIDE), F32)
+
+    @pl.when(quad == 0)
+    def _():
+        scores[...] = jnp.where(row >= col, nt(c_ref[...], b_ref[...]), 0.0)
+
+    entering = state[quad]
+    st_ref[0] = entering
+    across = nn(twice(c_ref[...]), stacked(parts(entering)))
+    within = scores[...]
+    ends, rights = [], []
+    for pair in range(QUAD // 2):
+        lanes = slice(128 * pair, 128 * pair + 128)
+        x = x_ref[:, lanes].astype(F32)
+        a1, a2, asel = pair_columns(acol_ref, pair, lane_low)
+        _, _, dsel = pair_columns(dtcol_ref, pair, lane_low)
+        u = x * dsel
+        m1 = within * jnp.exp(jnp.minimum(a1 - arow_ref[0, 2 * pair : 2 * pair + 1, :], 0.0))
+        m2 = within * jnp.exp(jnp.minimum(a2 - arow_ref[0, 2 * pair + 1 : 2 * pair + 2, :], 0.0))
+        both = jnp.concatenate([m1.astype(BF16), m2.astype(BF16)], axis=1)
+        y = nn(both, two_heads(u.astype(BF16), lane_low))
+        y_ref[:, lanes] = y + jnp.exp(asel) * across[:, lanes] + skip_ref[:, lanes] * x
+        last = asel[CHUNK - 1 : CHUNK, :]
+        rights.append(jnp.exp(last - asel) * u)
+        ends.append(jnp.exp(last))
+    added = nn(twice(bt_ref[...]), stacked(parts(jnp.concatenate(rights, axis=1))))
+    state[quad] = jnp.concatenate(ends, axis=1) * entering + added
+
+
+def scan_backward(per_seq, quads, x_ref, dy_ref, b_ref, c_ref, ct_ref, acol_ref, dtcol_ref, arow_ref, skip_ref, st_ref, pick_ref,
+                  dx_ref, db_ref, dc_ref, small_ref, dskip_ref, grads, scores, scores_t, dscores):
+    step, quad = pl.program_id(0), pl.program_id(1)
+    row = lax.broadcasted_iota(jnp.int32, (CHUNK, CHUNK), 0)
+    col = lax.broadcasted_iota(jnp.int32, (CHUNK, CHUNK), 1)
+    lane_low = col < HEADDIM
+
+    @pl.when(lax.rem(step, per_seq) == 0)
+    def _():
+        grads[quad] = jnp.zeros((CHUNK, WIDE), F32)
+
+    @pl.when(quad == 0)
+    def _():
+        scores[...] = jnp.where(row >= col, nt(c_ref[...], b_ref[...]), 0.0)
+        scores_t[...] = jnp.where(row <= col, nt(b_ref[...], c_ref[...]), 0.0)
+        dscores[...] = jnp.zeros_like(dscores)
+        db_ref[...] = jnp.zeros_like(db_ref)
+        dc_ref[...] = jnp.zeros_like(dc_ref)
+
+    leaving = grads[quad]
+    leaving_parts = parts(leaving)
+    entering = st_ref[0]
+    entering_parts = parts(entering)
+    across = nn(twice(c_ref[...]), stacked(entering_parts))
+    from_state = nn(twice(b_ref[...]), stacked(leaving_parts))
+    kept = jnp.sum(leaving * entering, axis=0, keepdims=True)
+    within, within_t = scores[...], scores_t[...]
+    dwithin = jnp.zeros((CHUNK, CHUNK), F32)
+    ends, rights, reads, his, los, steps = [], [], [], [], [], []
+    for pair in range(QUAD // 2):
+        lanes = slice(128 * pair, 128 * pair + 128)
+        x = x_ref[:, lanes].astype(F32)
+        dy = dy_ref[:, lanes]
+        dy_low = dy.astype(BF16)
+        dy_back = dy_low.astype(F32)
+        a1, a2, asel = pair_columns(acol_ref, pair, lane_low)
+        _, _, dsel = pair_columns(dtcol_ref, pair, lane_low)
+        r1 = arow_ref[0, 2 * pair : 2 * pair + 1, :]
+        r2 = arow_ref[0, 2 * pair + 1 : 2 * pair + 2, :]
+        d1, d2 = a1 - r1, a2 - r2
+        l1, l2 = jnp.exp(jnp.minimum(d1, 0.0)), jnp.exp(jnp.minimum(d2, 0.0))
+        t1, t2 = jnp.exp(jnp.minimum(-d1, 0.0)), jnp.exp(jnp.minimum(-d2, 0.0))
+        u = x * dsel
+        u_low = u.astype(BF16)
+        u_back = u_low.astype(F32)
+        dy_two = two_heads(dy_low, lane_low)
+        both = jnp.concatenate([(within * l1).astype(BF16), (within * l2).astype(BF16)], axis=1)
+        both_t = jnp.concatenate([(within_t * t1).astype(BF16), (within_t * t2).astype(BF16)], axis=1)
+        y = nn(both, two_heads(u_low, lane_low))
+        du = nn(both_t, dy_two)
+        w = nt(stacked((dy_two, two_heads((dy - dy_back).astype(BF16), lane_low)), 1), twice(u_low))
+        dwithin = dwithin + l1 * w[:CHUNK] + l2 * w[CHUNK:]
+        last = asel[CHUNK - 1 : CHUNK, :]
+        last_decay = jnp.exp(last)
+        into = jnp.exp(asel)
+        out_of = jnp.exp(last - asel)
+        du_state = out_of * from_state[:, lanes]
+        du_all = du + du_state
+        dx_ref[:, lanes] = dsel * du_all + skip_ref[:, lanes] * dy
+        passed = u * du_state
+        final = jnp.sum(passed, axis=0, keepdims=True) + last_decay * kept[:, lanes]
+        read = dy * into
+        da = dy_back * y + read * across[:, lanes] - u_back * du - passed
+        da = da + jnp.where(row == CHUNK - 1, final, 0.0)
+        da_hi = da.astype(BF16)
+        his.append(da_hi)
+        los.append((da - da_hi.astype(F32)).astype(BF16))
+        steps.append((x * du_all).astype(BF16))
+        reads.append(read)
+        rights.append(out_of * u)
+        ends.append(last_decay)
+        dskip_ref[0, :, lanes] = jnp.sum((dy * x).reshape(CHUNK // 8, 8, 128), axis=0)
+    read = parts(jnp.concatenate(reads, axis=1))
+    right = parts(jnp.concatenate(rights, axis=1))
+    dscores[...] += dwithin
+    dc_ref[...] += nt_parts(read, entering_parts)
+    db_ref[...] += nt_parts(right, leaving_parts)
+    grads[quad] = jnp.concatenate(ends, axis=1) * leaving + nn(twice(ct_ref[...]), stacked(read))
+    small_ref[0] = nn(jnp.concatenate(his + los + steps, axis=1), pick_ref[...])
+
+    @pl.when(quad == quads - 1)
+    def _():
+        total = jnp.where(row >= col, dscores[...], 0.0)
+        dc_ref[...] += nn(stacked(parts(total), 1), twice(b_ref[...], 0))
+        db_ref[...] += nn(stacked(parts(total.T), 1), twice(c_ref[...], 0))
+
+
+def scan_inputs(maps, log_decay, step_size):
+    tokens, heads = step_size.shape
+    quads = heads // QUAD
+    columns = lambda v: v.reshape(tokens, quads, QUAD).transpose(1, 0, 2)
+    rows = log_decay.T.reshape(quads, QUAD, tokens)
+    half = maps.shape[1] // 2
+    return maps[:, :half], maps[:, half:], columns(log_decay), columns(step_size), rows
+
+
+def run_forward(values, maps, log_decay, step_size, skip_lanes):
+    tokens, inner = values.shape
+    quads, chunks = inner // WIDE, tokens // CHUNK
+    enter, read, acol, dtcol, arow = scan_inputs(maps, log_decay, step_size)
+    tall = lambda: pl.BlockSpec((CHUNK, WIDE), lambda i, q: (i, q))
+    thin = lambda: pl.BlockSpec((CHUNK, CHUNK), lambda i, q: (i, 0))
+    cols = lambda: pl.BlockSpec((1, CHUNK, QUAD), lambda i, q: (q, i, 0))
+    return pl.pallas_call(
+        partial(scan_forward, SEQ // CHUNK),
+        grid=(chunks, quads),
+        in_specs=[tall(), thin(), thin(), pl.BlockSpec((CHUNK, CHUNK), lambda i, q: (0, i)), cols(), cols(),
+                  pl.BlockSpec((1, QUAD, CHUNK), lambda i, q: (q, 0, i)), pl.BlockSpec((1, WIDE), lambda i, q: (0, q))],
+        out_specs=[tall(), pl.BlockSpec((1, CHUNK, WIDE), lambda i, q: (i, 0, q))],
+        out_shape=[jax.ShapeDtypeStruct((tokens, inner), F32), jax.ShapeDtypeStruct((chunks, CHUNK, inner), F32)],
+        scratch_shapes=[pltpu.VMEM((quads, CHUNK, WIDE), F32), pltpu.VMEM((CHUNK, CHUNK), F32)],
+        compiler_params=pltpu.CompilerParams(vmem_limit_bytes=32 * 2**20),
+        cost_estimate=pl.CostEstimate(flops=tokens * inner * 1024, bytes_accessed=tokens * inner * 10, transcendentals=tokens * inner * 4),
+        name="scan_forward",
+    )(values, enter, read, enter.T, acol, dtcol, arow, skip_lanes)
+
+
+def run_backward(values, dmixed, maps, log_decay, step_size, skip_lanes, states):
+    tokens, inner = values.shape
+    quads, chunks = inner // WIDE, tokens // CHUNK
+    enter, read, acol, dtcol, arow = scan_inputs(maps, log_decay, step_size)
+    lane_head = jnp.arange(WIDE)[:, None] // HEADDIM
+    pick = lambda base: (lane_head + base == jnp.arange(128)[None, :]).astype(BF16)
+    picks = jnp.concatenate([pick(0), pick(0), pick(QUAD)], axis=0)
+    end = chunks - 1
+    tall = lambda: pl.BlockSpec((CHUNK, WIDE), lambda i, q: (end - i, q))
+    thin = lambda: pl.BlockSpec((CHUNK, CHUNK), lambda i, q: (end - i, 0))
+    cols = lambda: pl.BlockSpec((1, CHUNK, QUAD), lambda i, q: (q, end - i, 0))
+    dx, db, dc, small, dskip = pl.pallas_call(
+        partial(scan_backward, SEQ // CHUNK, quads),
+        grid=(chunks, quads),
+        in_specs=[tall(), tall(), thin(), thin(), pl.BlockSpec((CHUNK, CHUNK), lambda i, q: (0, end - i)), cols(), cols(),
+                  pl.BlockSpec((1, QUAD, CHUNK), lambda i, q: (q, 0, end - i)), pl.BlockSpec((1, WIDE), lambda i, q: (0, q)),
+                  pl.BlockSpec((1, CHUNK, WIDE), lambda i, q: (end - i, 0, q)), pl.BlockSpec((3 * WIDE, 128), lambda i, q: (0, 0))],
+        out_specs=[tall(), thin(), thin(), pl.BlockSpec((1, CHUNK, 128), lambda i, q: (q, end - i, 0)),
+                   pl.BlockSpec((1, 8, WIDE), lambda i, q: (end - i, 0, q))],
+        out_shape=[jax.ShapeDtypeStruct((tokens, inner), F32), jax.ShapeDtypeStruct((tokens, CHUNK), F32),
+                   jax.ShapeDtypeStruct((tokens, CHUNK), F32), jax.ShapeDtypeStruct((quads, tokens, 128), F32),
+                   jax.ShapeDtypeStruct((chunks, 8, inner), F32)],
+        scratch_shapes=[pltpu.VMEM((quads, CHUNK, WIDE), F32)] + [pltpu.VMEM((CHUNK, CHUNK), F32)] * 3,
+        compiler_params=pltpu.CompilerParams(vmem_limit_bytes=32 * 2**20),
+        cost_estimate=pl.CostEstimate(flops=tokens * inner * 2560, bytes_accessed=tokens * inner * 12, transcendentals=tokens * inner * 8),
+        name="scan_backward",
+    )(values, dmixed, enter, read, read.T, acol, dtcol, arow, skip_lanes, states, picks)
+    per_head = lambda part: part.transpose(1, 0, 2).reshape(tokens, quads * QUAD)
+    dlog = per_head(small[:, :, :QUAD])
+    dstep = per_head(small[:, :, QUAD : 2 * QUAD])
+    dskip = jnp.sum(dskip.reshape(chunks * 8, inner // HEADDIM, HEADDIM), axis=(0, 2))
+    return dx, jnp.concatenate([db, dc], axis=1), dlog, dstep, dskip
+
+
+def chunk_sums(v, lower):
+    tokens, heads = v.shape
+    framed = v.reshape(tokens // CHUNK, CHUNK, heads)
+    ones = jnp.tril(jnp.ones((CHUNK, CHUNK), F32))
+    ones = ones if lower else ones.T
+    return jnp.einsum("ts,csh->cth", ones, framed, precision=lax.Precision.HIGHEST).reshape(tokens, heads)
+
+
+def to_sequences(block):
+    me = lax.axis_index("tp")
+    rows = block.shape[0] // 2
+    mine = lax.dynamic_slice_in_dim(block, me * rows, rows, 0)
+    other = lax.dynamic_slice_in_dim(block, (1 - me) * rows, rows, 0)
+    came = lax.ppermute(other, "tp", [(0, 1), (1, 0)])
+    first = me == 0
+    return jnp.concatenate([jnp.where(first, mine, came), jnp.where(first, came, mine)], axis=1)
+
+
+def to_features(block):
+    me = lax.axis_index("tp")
+    cols = block.shape[1] // 2
+    mine = lax.dynamic_slice_in_dim(block, me * cols, cols, 1)
+    other = lax.dynamic_slice_in_dim(block, (1 - me) * cols, cols, 1)
+    came = lax.ppermute(other, "tp", [(0, 1), (1, 0)])
+    first = me == 0
+    return jnp.concatenate([jnp.where(first, mine, came), jnp.where(first, came, mine)], axis=0)
+
+
+def gather_columns(shards):
+    widths = [shard.shape[1] for shard in shards]
+    wide = lax.all_gather(jnp.concatenate(shards, axis=1), "tp", axis=0)
+    pieces, at = [], 0
+    for width in widths:
+        pieces += [wide[part, :, at : at + width] for part in range(wide.shape[0])]
+        at += width
+    return lax.all_gather(jnp.concatenate(pieces, axis=1), "dp", axis=0, tiled=True)
+
+
+def scatter_columns(whole, widths, tp):
+    rows = lax.psum_scatter(whole, "dp", scatter_dimension=0, tiled=True)
+    pieces, at = [], 0
+    for width in widths:
+        pieces.append(rows[:, at : at + width * tp].reshape(rows.shape[0], tp, width))
+        at += width * tp
+    mine = lax.psum_scatter(jnp.concatenate(pieces, axis=2).transpose(1, 0, 2), "tp", scatter_dimension=0, tiled=True)[0]
+    outs, at = [], 0
+    for width in widths:
+        outs.append(mine[:, at : at + width])
+        at += width
+    return outs
+
+
+def by_sequences(
+    tp,
+    resid_in,
+    norm_gain,
+    proj_gate,
+    proj_value,
+    proj_state,
+    proj_step,
+    conv_value,
+    value_bias,
+    conv_state,
+    state_bias,
+    step_bias,
+    decay_log,
+    skip_gain,
+    gate_gain,
+    proj_out,
+    cotangent,
+):
+    small_in = [norm_gain.astype(F32), conv_value, value_bias, conv_state, state_bias, step_bias, decay_log, skip_gain, gate_gain]
+    packed = lax.all_gather(jnp.concatenate([v.reshape(-1) for v in small_in]), "tp", axis=0)
+    fulls, at = [], 0
+    for v in small_in:
+        piece = packed[:, at : at + v.size].reshape((tp,) + v.shape)
+        at += v.size
+        fulls.append(piece.reshape(-1) if v.ndim == 1 else piece.transpose(1, 0, 2).reshape(v.shape[0], -1))
+    gain, conv_v, bias_v, conv_s, bias_s, bias_step, log_rate, skip, gain_out = fulls
+
+    resid = to_sequences(resid_in).astype(F32)
+    low_w = gather_columns([proj_value, proj_state, proj_step])
+    gate_w = gather_columns([proj_gate])
+    out_rows = lax.all_gather(proj_out, "tp", axis=0, tiled=True)
+    out_w = lax.all_gather(out_rows, "dp", axis=1, tiled=True)
+    cot_low = to_sequences(cotangent)
+
+    tokens = resid.shape[0]
+    seqs = tokens // SEQ
+    inner = gate_w.shape[1]
+    states = conv_s.shape[1]
+    value_w, rest_w = low_w[:, :inner], low_w[:, inner:]
+
+    inv_rms = lax.rsqrt(jnp.mean(resid * resid, axis=-1, keepdims=True) + epsilon)
+    unit_rows = resid * inv_rms
+    normed_in = (unit_rows * gain).astype(BF16)
+    value_raw = product(normed_in, value_w)
+    rest_raw = product(normed_in, rest_w)
+    state_raw, step_raw = rest_raw[:, :states], rest_raw[:, states:]
+
+    def conv_act(raw, kernel, kernel_bias):
+        framed = raw.reshape(seqs, SEQ, raw.shape[1])
+        convolved = jax.vmap(causal_conv, (0, None, None))(framed, kernel, kernel_bias)
+        return jax.nn.silu(convolved).reshape(raw.shape)
+
+    value_act, value_pull = jax.vjp(conv_act, value_raw, conv_v, bias_v)
+    values = value_act.astype(BF16)
+    state_act, state_pull = jax.vjp(conv_act, state_raw, conv_s, bias_s)
+    maps = state_act.astype(BF16)
+    step_size, step_pull = jax.vjp(lambda v: jax.nn.softplus(v + bias_step), step_raw)
+    rate = -jnp.exp(log_rate)
+    log_decay = chunk_sums(step_size * rate, True)
+    skip_lanes = jnp.repeat(skip, HEADDIM)[None, :]
+    mixed, entering = run_forward(values, maps, log_decay, step_size, skip_lanes)
+
+    gate_raw = product(normed_in, gate_w)
+    gated, gate_pull = jax.vjp(gating, mixed, gate_raw)
+    squares = jnp.sum(gated * gated, axis=-1, keepdims=True)
+    gate_scale = lax.rsqrt(squares / inner + epsilon)
+    scaled = gated * gate_scale
+    normed_out = (scaled * gain_out).astype(BF16)
+    block_out = to_features((resid + product(normed_out, out_w)).astype(BF16))
+    normed_grad = product_right(cot_low, out_w)
+    out_grad = product_left(normed_out, cot_low)
+    gate_gain_grad = jnp.sum(normed_grad * scaled, axis=0)
+    weighted = normed_grad * gain_out
+    crossed = jnp.sum(weighted * gated, axis=-1, keepdims=True)
+    cubed = gate_scale * gate_scale * gate_scale
+    gated_grad = weighted * gate_scale - gated * cubed * (crossed / inner)
+    mixed_grad, gate_raw_grad = gate_pull(gated_grad)
+    gate_low = gate_raw_grad.astype(BF16)
+    gate_w_grad = product_left(normed_in, gate_low)
+    mixed_grad, gate_w_grad, out_grad = lax.optimization_barrier((mixed_grad, gate_w_grad, out_grad))
+
+    values_grad, maps_grad, dlog, dstep, skip_grad = run_backward(
+        values, mixed_grad, maps, log_decay, step_size, skip_lanes, entering
+    )
+    summed = chunk_sums(dlog, False)
+    decay_grad = rate * jnp.sum(summed * step_size, axis=0)
+    (step_grad,) = step_pull(dstep + summed * rate)
+    step_bias_grad = jnp.sum(step_grad, axis=0)
+    value_raw_grad, conv_value_grad, value_bias_grad = value_pull(values_grad)
+    state_raw_grad, conv_state_grad, state_bias_grad = state_pull(maps_grad)
+    rest_low = jnp.concatenate([state_raw_grad.astype(BF16), step_grad.astype(BF16)], axis=1)
+    value_low = value_raw_grad.astype(BF16)
+    value_w_grad = product_left(normed_in, value_low)
+    rest_w_grad = product_left(normed_in, rest_low)
+    input_grad = (
+        product_right(gate_low, gate_w) + product_right(value_low, value_w) + product_right(rest_low, rest_w)
+    )
+    gain_grad = jnp.sum(input_grad * unit_rows, axis=0)
+    pulled = input_grad * gain
+    crossed_rows = jnp.sum(pulled * resid, axis=-1, keepdims=True)
+    rms_cubed = inv_rms * inv_rms * inv_rms
+    grad_in = (
+        cot_low.astype(F32) + pulled * inv_rms - resid * rms_cubed * (crossed_rows / resid.shape[1])
+    ).astype(BF16)
+    grad_in = to_features(grad_in)
+
+    (gate_mine,) = scatter_columns(gate_w_grad, [proj_gate.shape[1]], tp)
+    value_mine, state_mine, step_mine = scatter_columns(
+        jnp.concatenate([value_w_grad, rest_w_grad], axis=1),
+        [proj_value.shape[1], proj_state.shape[1], proj_step.shape[1]],
+        tp,
+    )
+    out_cols = lax.psum_scatter(out_grad, "dp", scatter_dimension=1, tiled=True)
+    out_mine = lax.psum_scatter(out_cols, "tp", scatter_dimension=0, tiled=True)
+
+    small_out = [gain_grad, conv_value_grad, value_bias_grad, conv_state_grad, state_bias_grad, step_bias_grad, decay_grad, skip_grad, gate_gain_grad]
+    split = [
+        v.reshape(tp, -1) if v.ndim == 1 else v.reshape(v.shape[0], tp, -1).transpose(1, 0, 2).reshape(tp, -1)
+        for v in small_out
+    ]
+    sums = lax.psum(jnp.concatenate(split, axis=1), ("dp", "tp"))
+    mine = lax.dynamic_slice_in_dim(sums, lax.axis_index("tp"), 1, 0)[0]
+    smalls, at = [], 0
+    for v in small_in:
+        smalls.append(mine[at : at + v.size].reshape(v.shape))
+        at += v.size
+    return (
+        block_out,
+        grad_in,
+        smalls[0],
+        gate_mine,
+        value_mine,
+        state_mine,
+        step_mine,
+        *smalls[1:],
+        out_mine,
+    )
+
+
 def solution(mesh):
+    tp = mesh.shape["tp"]
+
+    def local(*args):
+        seqs = args[0].shape[0] // SEQ
+        if seqs % tp == 0 and tp == 2:
+            return by_sequences(tp, *args)
+        return by_heads(*args)
+
     return jax.shard_map(
         local,
         mesh=mesh,

time: 2540 us -> 924 us (0.36)
  waiting for transfers between devices: 773 us -> 114 us
  matrix products: 800 us -> 155 us
  local copies, waits for them, and re-layouts: 396 us -> 83.6 us
  other arithmetic: 385 us -> 225 us
  Pallas kernels: 0 us -> 136 us
  blocking collectives: 128 us -> 185 us
  loops' own time: 27.3 us -> 0 us
    dot_general x112 -> x2, matrix products: 591 us -> 1.47 us  [chunk_sums(): jnp.einsum('ts,csh->cth', ones, framed, precision=lax.Precision.HIGHEST)]
    psum x1 -> x0, waiting for transfers between devices: 300 us -> none  [local(): input_whole = lax.psum(input_terms, 'tp')]
    reduce_scatter x6 -> x5, waiting for transfers between devices: 393 us -> 113 us  [the longest x2 64.4 us: scatter_columns(): rows = lax.psum_scatter(whole, 'dp', scatter_dimension=0, tiled=True)]
    pallas_call x0 -> x2, Pallas kernels: none -> 136 us  [the longest x1 88.5 us: run_backward(): pl.pallas_call(partial(scan_backward, SEQ // CHUNK, quads), grid=(chunks,...]
    another operation x82 -> x0, other arithmetic: 98.3 us -> none
    all_gather x6 -> x3, waiting for transfers between devices: 77.7 us -> 0.01 us  [the longest x2 0.01 us: gather_columns(): lax.all_gather(jnp.concatenate(pieces, axis=1), 'dp', axis=0, tiled=True)]
    squeeze x32 -> x3, local copies, waits for them, and re-layouts: 73.3 us -> 0.03 us  [gather_columns(): pieces += [wide[part, :, at:at + width] for part in range(wide.shape[0])]]
    another operation x108 -> x4, local copies, waits for them, and re-layouts: 66.7 us -> 2.79 us  [the longest x2 2.71 us: scan_inputs(): columns = lambda v: v.reshape(tokens, quads, QUAD).transpose(1, 0, 2)]
  transfers between devices with their start and end apart: 14 -> 13, of which waited for: 6 -> 4; matrix products, arithmetic and copies ran while one was open for 28% -> 37% of each run, Pallas kernels for 0% -> 5%
where the time goes in v1:
time: 924 us; the launch traced here: 920 us
  other arithmetic  225 us (24%)
  blocking collectives  185 us (20%)
  matrix products  155 us (17%)
  Pallas kernels  136 us (15%)
  waiting for transfers between devices  114 us (12%)
  local copies, waits for them, and re-layouts  83.6 us (9%)
  between operations  16 us (2%)
    all_gather x1, blocking collectives, by_sequences(): out_rows = lax.all_gather(proj_out, 'tp', axis=0, tiled=True)  89.3 us
    pallas_call x1, Pallas kernels, run_backward(): pl.pallas_call(partial(scan_backward, SEQ // CHUNK, quads), grid=(chunks,...  88.5 us
    psum x1, blocking collectives, by_sequences(): sums = lax.psum(jnp.concatenate(split, axis=1), ('dp', 'tp'))  73.2 us
    reduce_scatter x2, waiting for transfers between devices, scatter_columns(): rows = lax.psum_scatter(whole, 'dp', scatter_dimension=0, tiled=True)  64.4 us
    dot_general x4, matrix products, product_right(): jnp.einsum('tc,kc->tk', matrix, factor, preferred_element_type=jnp.float32)  55.5 us
    dot_general x4, matrix products, product(): return jnp.dot(matrix, factor, preferred_element_type=jnp.float32)  53.4 us
    reduce_sum x2, other arithmetic, causal_conv(): summed = summed + kernel[offset][None, :] * padded[offset:offset + length]  48.6 us
    pallas_call x1, Pallas kernels, run_forward(): pl.pallas_call(partial(scan_forward, SEQ // CHUNK), grid=(chunks, quads),...  47.4 us
  transfers between devices with their start and end apart: 13, of which 4 were waited for; matrix products, arithmetic and copies ran while one was open for 37% of the time, Pallas kernels for 5%

profile of v1, /device:TPU:0, one launch (start us, length us, event | category | flops | bytes accessed | tf_op | source)
XLA Modules:
  0.0 919.7 jit_solution(6870451702130857922)
XLA Ops:
  8.9 7.8 all-gather.1
  17.7 5.9 all-gather.2
  30.7 89.3 %all_gather.38 = bf16[2048,64]{0,1:T(8,128)(2,1)} all-gather(bf16[1024,64]{0,1:T(8,128)(2,1)S(1)} %copy-done.42), channel_id=1, replica_groups=mesh['dp'=16,'tp'=2] {'tp'}, dimensions={0}, use_global_device_ids=true | all-gather | bytes 393216 | tf_op jit(solution)/shard_map/all_gather | solution.py:568
  122.1 8.7 all-reduce.18
  152.9 12.3 %fusion.22 = f32[2048,2048]{1,0:T(8,128)} fusion(bf16[1024,2336]{1,0:T(8,128)(2,1)S(1)} %bitcast.217, f32[1024]{0:T(1024)S(1)} %bitcast.231, f32[2048]{0:T(1024)S(1)} %get-tuple-element.178, bf16[2048,512]{1,0:T(8,128)(2,1)S(1)} %copy-done.16, bf16[2048,512]{1,0:T(8,128)(2,1)S(1)} %get-tuple-element.136), kind=kOutput, calls=%fused_computation.59 | convolution fusion | flops 8604614656 | bytes 25178112 | tf_op jit(solution)/shard_map/dot_general | solution.py:71
  165.2 33.0 %fusion.19 = (bf16[2048,2048]{1,0:T(8,128)(2,1)}, f32[1,2048,2048]{2,1,0:T(8,128)}) fusion(f32[2048,2048]{1,0:T(8,128)} %fusion.22, f32[2048]{0:T(1024)S(1)} %bitcast.222, f32[2048]{0:T(1024)S(1)} %bitcast.224, f32[2048]{0:T(1024)S(1)} %bitcast.226, f32[1,2048,2048]{2,1,0:T(8,128)} %bitcast.194, f32[2048]{0:T(1024)S(1)} %bitcast.220, f32[2048]{0:T(1024)S(1)} %bitcast.238), kind=kLoop, calls=%fused_computation.50 | loop fusion | flops 54525952 | bytes 58761216 | tf_op jit(solution)/shard_map/convert_element_type | solution.py:591
  212.6 47.4 %scan_forward.1 = (f32[2048,2048]{1,0:T(8,128)}, f32[16,128,2048]{2,1,0:T(8,128)}) custom-call(bf16[2048,2048]{1,0:T(8,128)(2,1)S(1)} %copy-done, bf16[2048,128]{1,0:T(8,128)(2,1)S(1)} %copy.113.b_ref, bf16[2048,128]{1,0:T(8,128)(2,1)S(1)} %copy.114.c_ref, bf16[128,2048]{1,0:T(8,128)(2,1)S(1)} %get-tuple-element.148.bt_ref, f32[4,2048,8]{2,1,0:T(8,128)S(1)} %bitcast.190, ...), custom_call_target="tpu_custom_call" | custom-call | flops 4294967296 | bytes 41943040 | tf_op jit(solution)/shard_map/scan_forward/pallas_call | solution.py:437
  260.7 23.3 %multiply_reduce_fusion.6 = (f32[2048]{0:T(1024)S(1)}, f32[2048,2048]{1,0:T(8,128)}, f32[2048,2048]{1,0:T(8,128)}) fusion(f32[2048,2048]{1,0:T(8,128)} %get-tuple-element.26, bf16[1024,2048]{1,0:T(8,128)(2,1)} %all-gather.9.cloned.1.call-done, f32[1024]{0:T(1024)} %bitcast.232, f32[2048]{0:T(1024)S(1)} %get-tuple-element.178, ...), kind=kOutput, calls=%fused_computation.22 | convolution fusion | flops 8633972736 | bytes 58740736 | tf_op jit(solution)/shard_map/dot_general | solution.py:71
  284.1 14.9 %fusion.28 = f32[2048,1024]{1,0:T(8,128)} fusion(bf16[2048,512]{1,0:T(8,128)(2,1)S(1)} %copy-done.27, bf16[2048,512]{1,0:T(8,128)(2,1)S(1)} %copy-done.26, f32[2048,2048]{1,0:T(8,128)} %get-tuple-element.119, f32[2048]{0:T(1024)S(1)} %bitcast.243, f32[2048]{0:T(1024)S(1)} %get-tuple-element.180), kind=kOutput, calls=%fused_computation.89 | convolution fusion | flops 8610906112 | bytes 29376512 | tf_op jit(solution)/shard_map/tk,tc->kc/dot_general | solution.py:75
  298.9 18.6 %multiply_reduce_fusion = (f32[2048]{0:T(1024)}, f32[2048]{0:T(1024)S(1)}, f32[2048,2048]{1,0:T(8,128)}) fusion(f32[2048,2048]{1,0:T(8,128)} %get-tuple-element.119, f32[2048]{0:T(1024)S(1)} %get-tuple-element.180, f32[2048]{0:T(1024)S(1)} %bitcast.244, bf16[2048,1024]{0,1:T(8,128)(2,1)} %all-gather.11.cloned.1.call-done, ...), kind=kOutput, calls=%fused_computation.14 | convolution fusion | flops 8623484928 | bytes 41975808 | tf_op jit(solution)/shard_map/tc,kc->tk/dot_general | solution.py:79
  317.6 32.7 %fusion.18 = (f32[2048,2048]{1,0:T(8,128)}, bf16[2048,2048]{1,0:T(8,128)(2,1)}) fusion(f32[2048]{0:T(1024)S(1)} %broadcast_multiply_fusion.8, f32[2048,2048]{1,0:T(8,128)} %get-tuple-element.119, f32[2048,2048]{1,0:T(8,128)} %get-tuple-element.186, f32[2048]{0:T(1024)S(1)} %get-tuple-element.179, f32[2048]{0:T(1024)S(1)} %bitcast.245, ...), kind=kLoop, calls=%fused_computation.46 | loop fusion | flops 75497472 | bytes 92307456 | tf_op jit(solution)/shard_map/transpose(jvp())/mul | solution.py:83
  350.3 13.9 %fusion.70 = f32[1024,2048]{1,0:T(8,128)} fusion(bf16[2048,2048]{1,0:T(8,128)(2,1)} %get-tuple-element.125, f32[1024]{0:T(1024)S(1)} %bitcast.233, f32[2048]{0:T(1024)S(1)} %get-tuple-element.178, bf16[2048,512]{1,0:T(8,128)(2,1)S(1)} %copy-done.17, bf16[2048,512]{1,0:T(8,128)(2,1)S(1)} %copy-done.13), kind=kOutput, calls=%fused_computation.191 | convolution fusion | flops 8604614656 | bytes 20983808 | tf_op jit(solution)/shard_map/tk,tc->kc/dot_general | solution.py:75
  372.7 88.5 %scan_backward.1 = (f32[2048,2048]{1,0:T(8,128)}, f32[2048,128]{1,0:T(8,128)S(1)}, f32[2048,128]{1,0:T(8,128)S(1)}, f32[4,2048,128]{2,1,0:T(8,128)S(1)}, f32[16,8,2048]{2,1,0:T(8,128)S(1)}) custom-call(bf16[2048,2048]{1,0:T(8,128)(2,1)} %get-tuple-element.122.x_ref, f32[2048,2048]{1,0:T(8,128)} %get-tuple-element.27.dy_ref, bf16[2048,128]{1,0:T(8,128)(2,1)S(1)} %copy-done.6, ...), custom_call_target="tpu_custom_call" | custom-call | flops 10737418240 | bytes 50331648 | tf_op jit(solution)/shard_map/scan_backward/pallas_call | solution.py:462
  471.2 6.7 multiply_reduce_fusion.9
  481.9 9.1 copy.138
  498.1 6.1 fusion.30
  508.3 41.9 %multiply_reduce_fusion.3 = (f32[2048]{0:T(1024)S(1)}, f32[2048]{0:T(1024)S(1)}, f32[2048]{0:T(1024)S(1)}, f32[2048]{0:T(1024)S(1)}, f32[2048]{0:T(1024)S(1)}, /*index=5*/f32[1,2048,2048]{2,1,0:T(8,128)}) fusion(f32[1,2048,2048]{2,1,0:T(8,128)} %bitcast.195, f32[2048,2048]{1,0:T(8,128)} %fusion.22, f32[1,2048,2048]{2,1,0:T(8,128)} %get-tuple-element.123, ...), kind=kLoop, calls=%fused_computation.17 | loop fusion | flops 75487232 | bytes 83927040 | tf_op jit(solution)/shard_map/transpose(jvp(vmap()))/reduce_sum | solution.py:26
  550.3 27.1 %broadcast_multiply_fusion = (f32[1,2048,2048]{2,1,0:T(8,128)}, f32[1,2048,2048]{2,1,0:T(8,128)}, f32[1,2048,2048]{2,1,0:T(8,128)}, f32[1,2048,2048]{2,1,0:T(8,128)}) fusion(f32[1,2048,2048]{2,1,0:T(8,128)} %get-tuple-element.117, f32[2048]{0:T(1024)S(1)} %bitcast.223, f32[2048]{0:T(1024)S(1)} %bitcast.221, f32[2048]{0:T(1024)S(1)} %bitcast.227, ...), kind=kLoop, calls=%fused_computation.45 | loop fusion | flops 16777216 | bytes 83918848 | tf_op jit(solution)/shard_map/transpose(jvp(vmap()))/mul | solution.py:26
  577.4 23.6 %fusion.17 = bf16[2048,2048]{1,0:T(8,128)(2,1)S(1)} fusion(f32[1,2048,2048]{2,1,0:T(8,128)} %get-tuple-element.127, f32[1,2048,2048]{2,1,0:T(8,128)} %get-tuple-element.128, f32[1,2048,2048]{2,1,0:T(8,128)} %get-tuple-element.129, f32[1,2048,2048]{2,1,0:T(8,128)} %get-tuple-element.126), kind=kLoop, calls=%fused_computation.43 | loop fusion | flops 16777216 | bytes 75497472 | tf_op jit(solution)/shard_map/convert_element_type | solution.py:629
  604.3 11.5 %fusion.68 = f32[1024,2048]{1,0:T(8,128)} fusion(bf16[2048,2048]{1,0:T(8,128)(2,1)S(1)} %fusion.17, f32[1024]{0:T(1024)S(1)} %bitcast.235, f32[2048]{0:T(1024)S(1)} %get-tuple-element.178, bf16[2048,512]{1,0:T(8,128)(2,1)S(1)} %copy-done.19, bf16[2048,512]{1,0:T(8,128)(2,1)S(1)} %copy-done.14), kind=kOutput, calls=%fused_computation.190 | convolution fusion | flops 8604614656 | bytes 20983808 | tf_op jit(solution)/shard_map/tk,tc->kc/dot_general | solution.py:75
  615.8 8.5 pad_maximum_fusion
  625.1 14.4 %fusion.12 = bf16[2048,1024]{1,0:T(8,128)(2,1)S(1)} fusion(bf16[2048,1024]{0,1:T(8,128)(2,1)} %all-gather.11.cloned.1.call-done, f32[2048,2048]{1,0:T(8,128)} %get-tuple-element.119, f32[2048]{0:T(1024)S(1)} %bitcast.246, f32[2048]{0:T(1024)S(1)} %copy-done.56, bf16[2048,512]{1,0:T(8,128)(2,1)} %copy-done.15, bf16[2048,512]{1,0:T(8,128)(2,1)S(1)} %copy-done.14), kind=kOutput, calls=%fused_computation.38 | convolution fusion | flops 8615100416 | bytes 29376512 | tf_op jit(solution)/shard_map/dot_general | solution.py:71
  642.9 16.6 %fusion.88 = f32[2048,1024]{1,0:T(8,128)} fusion(bf16[2048,2048]{1,0:T(8,128)(2,1)} %get-tuple-element.125, bf16[1024,2048]{1,0:T(8,128)(2,1)} %all-gather.9.cloned.1.call-done), kind=kOutput, calls=%fused_computation.201 | convolution fusion | flops 8589934592 | bytes 20971520 | tf_op jit(solution)/shard_map/tc,kc->tk/dot_general | solution.py:79
  659.5 11.6 %fusion.20 = f32[2048,1024]{1,0:T(8,128)} fusion(bf16[2048,2048]{1,0:T(8,128)(2,1)S(1)} %bitcast.198, bf16[1024,2336]{1,0:T(8,128)(2,1)S(1)} %bitcast.219), kind=kOutput, calls=%fused_computation.57 | convolution fusion | flops 8589934592 | bytes 20971520 | tf_op jit(solution)/shard_map/tc,kc->tk/dot_general | solution.py:79
  671.1 8.7 fusion.10
  679.8 4.8 fusion.15
  693.8 73.2 %psum.7 = f32[2,7344]{1,0:T(2,128)S(1)} all-reduce(f32[2,7344]{1,0:T(2,128)S(1)} %concatenate.56), channel_id=1, replica_groups=mesh['dp'=16,'tp'=2] {'dp','tp'}, use_global_device_ids=true, to_apply=%region_20.21 | all-reduce | flops 14688 | bytes 117504 | tf_op jit(solution)/shard_map/psum | solution.py:658
  774.7 5.2 broadcast_select_fusion.5
  784.6 64.4 %reduce-scatter.9.cloned.1.call-done = f32[64,2048]{1,0:T(8,128)} async-done(((f32[1024,2048]{1,0:T(8,128)}), f32[64,2048]{1,0:T(8,128)}) %reduce-scatter.9.cloned.1.call-update) | async-done | bytes 524304 | tf_op jit(solution)/shard_map/reduce_scatter | solution.py:524
  857.2 14.0 %reduce-scatter.17.cloned.1.call-done = f32[1024,64]{1,0:T(8,128)} async-done(((f32[2048,64]{1,0:T(8,128)}), f32[1024,64]{1,0:T(8,128)}) %reduce-scatter.17.cloned.1.call-update) | async-done | bytes 262160 | tf_op jit(solution)/shard_map/reduce_scatter | solution.py:651
  873.2 22.4 %reduce-scatter.15.cloned.1.call-done = f32[1,64,1168]{1,2,0:T(8,128)} async-done(((f32[2,64,1168]{1,2,0:T(8,128)}), f32[1,64,1168]{1,2,0:T(8,128)}) %reduce-scatter.15.cloned.1.call-update) | async-done | bytes 299024 | tf_op jit(solution)/shard_map/reduce_scatter | solution.py:529
  900.4 12.6 %reduce-scatter.11.cloned.1.call-done = f32[1,64,1024]{2,1,0:T(8,128)} async-done(((f32[2,64,1024]{2,1,0:T(8,128)}), f32[1,64,1024]{2,1,0:T(8,128)}) %reduce-scatter.11.cloned.1.call-update) | async-done | bytes 262160 | tf_op jit(solution)/shard_map/reduce_scatter | solution.py:529
  (332 shorter events, 124.9 us)
Async XLA Ops:
  7.2 136.4 %all-gather.7.cloned.1.call-start = ((), (), s32[]{:S(2)}) async-start(), calls=%async_computation.6 | async-start | bytes 5292032 | tf_op jit(solution)/shard_map/all_gather | solution.py:520
  17.6 243.1 %all-gather.9.cloned.1.call-start = ((), (), s32[]{:S(2)}) async-start(), calls=%async_computation.7 | async-start | bytes 4456448 | tf_op jit(solution)/shard_map/all_gather | solution.py:520
  23.6 96.5 %copy-start.59 = (f32[4,1024]{1,0:T(4,128)S(1)}, f32[4,1024]{1,0:T(4,128)}, u32[]{:S(2)}) copy-start(f32[4,1024]{1,0:T(4,128)} %param.22) | copy-start | bytes 49156
  23.6 96.5 %copy-start.88 = (u32[32]{0:T(128)S(1)}, u32[32]{0:T(128)}, u32[]{:S(2)}) copy-start(u32[32]{0:T(128)} %constant.109) | copy-start | bytes 388
  23.6 97.8 %copy-start.74 = (f32[1024]{0:T(1024)S(1)}, f32[1024]{0:T(1024)}, u32[]{:S(2)}) copy-start(f32[1024]{0:T(1024)} %param.23) | copy-start | bytes 12292
  23.6 97.8 %copy-start.75 = (f32[1024]{0:T(1024)S(1)}, f32[1024]{0:T(1024)}, u32[]{:S(2)}) copy-start(f32[1024]{0:T(1024)} %param.29) | copy-start | bytes 12292
  23.6 97.7 %copy-start.80 = (f32[4,128]{1,0:T(4,128)S(1)}, f32[4,128]{1,0:T(4,128)}, u32[]{:S(2)}) copy-start(f32[4,128]{1,0:T(4,128)} %param.24) | copy-start | bytes 6148
  23.6 97.7 %copy-start.81 = (bf16[512]{0:T(512)(128)(2,1)S(1)}, bf16[512]{0:T(512)(128)(2,1)}, u32[]{:S(2)}) copy-start(bf16[512]{0:T(512)(128)(2,1)} %param.17) | copy-start | bytes 3076
  23.6 97.7 %copy-start.84 = (f32[128]{0:T(128)S(1)}, f32[128]{0:T(128)}, u32[]{:S(2)}) copy-start(f32[128]{0:T(128)} %param.25) | copy-start | bytes 1540
  23.7 97.7 %copy-start.85 = (f32[16]{0:T(128)S(1)}, f32[16]{0:T(128)}, u32[]{:S(2)}) copy-start(f32[16]{0:T(128)} %param.26) | copy-start | bytes 196
  23.7 97.7 %copy-start.86 = (f32[16]{0:T(128)S(1)}, f32[16]{0:T(128)}, u32[]{:S(2)}) copy-start(f32[16]{0:T(128)} %param.27) | copy-start | bytes 196
  23.7 97.7 %copy-start.87 = (f32[16]{0:T(128)S(1)}, f32[16]{0:T(128)}, u32[]{:S(2)}) copy-start(f32[16]{0:T(128)} %param.28) | copy-start | bytes 196
  24.4 274.5 %all-gather.11.cloned.1.call-start = ((), (), s32[]{:S(2)}) async-start(), calls=%async_computation.8 | async-start | bytes 4456448 | tf_op jit(solution)/shard_map/all_gather | solution.py:569
  26.4 106.2 %collective-permute-start = (bf16[2048,512]{1,0:T(8,128)(2,1)S(1)}, bf16[2048,512]{1,0:T(8,128)(2,1)}, u32[]{:S(2)}, u32[]{:S(2)}) collective-permute-start(bf16[2048,512]{1,0:T(8,128)(2,1)S(1)} %constant_dynamic-slice_fusion.4), channel_id=1, source_target_pairs={{0,1},{1,0},{2,3},{3,2},{4,5},{5,4},{6,7},{7,6},{8,9},{9,8},{10,11... | collective-permute-start | bytes 6291464 | tf_op jit(solution)/shard_map/ppermute | solution.py:498
  29.7 109.5 %collective-permute-start.2 = (bf16[2048,512]{1,0:T(8,128)(2,1)}, bf16[2048,512]{1,0:T(8,128)(2,1)}, u32[]{:S(2)}, u32[]{:S(2)}) collective-permute-start(bf16[2048,512]{1,0:T(8,128)(2,1)} %constant_dynamic-slice_fusion.2), channel_id=1, source_target_pairs={{0,1},{1,0},{2,3},{3,2},{4,5},{5,4},{6,7},{7,6},{8,9},{9,8},{10,11... | collective-permute-start | bytes 6291464 | tf_op jit(solution)/shard_map/ppermute | solution.py:498
  120.0 569.8 %reduce-scatter.19.cloned.1.call-start = ((), (), s32[]{:S(2)}) async-start(), calls=%async_computation.14 | async-start | bytes 8912896
  132.2 33.0 %copy-start.43 = (f32[1,2,1024]{2,0,1:T(1,128)}, f32[1,2,1024]{2,0,1:T(1,128)S(1)}, u32[]{:S(2)}) copy-start(f32[1,2,1024]{2,0,1:T(1,128)S(1)} %get-tuple-element.173) | copy-start | bytes 24580
  132.2 33.0 %copy-start.45 = (f32[1,2,1024]{2,0,1:T(1,128)}, f32[1,2,1024]{2,0,1:T(1,128)S(1)}, u32[]{:S(2)}) copy-start(f32[1,2,1024]{2,0,1:T(1,128)S(1)} %get-tuple-element.174) | copy-start | bytes 24580
  165.2 33.4 %copy-start.36 = (bf16[2048,128]{0,1:T(8,128)(2,1)S(1)}, bf16[2048,128]{0,1:T(8,128)(2,1)}, u32[]{:S(2)}) copy-start(bf16[2048,128]{0,1:T(8,128)(2,1)} %get-tuple-element.150) | copy-start | bytes 1572868
  165.2 33.7 %copy-start.35 = (bf16[2048,128]{0,1:T(8,128)(2,1)S(1)}, bf16[2048,128]{0,1:T(8,128)(2,1)}, u32[]{:S(2)}) copy-start(bf16[2048,128]{0,1:T(8,128)(2,1)} %get-tuple-element.149) | copy-start | bytes 1572868
  284.0 33.6 %copy-start.55 = (f32[2048]{0:T(1024)}, f32[2048]{0:T(1024)S(1)}, u32[]{:S(2)}) copy-start(f32[2048]{0:T(1024)S(1)} %get-tuple-element.180) | copy-start | bytes 24580
  491.1 279.2 %reduce-scatter.13.cloned.1.call-start = ((), (), s32[]{:S(2)}) async-start(), calls=%async_computation.11 | async-start | bytes 10584064 | tf_op jit(solution)/shard_map/reduce_scatter | solution.py:524
  508.3 42.0 %copy-start.44 = (f32[1,2,1024]{2,0,1:T(1,128)S(1)}, f32[1,2,1024]{2,0,1:T(1,128)}, u32[]{:S(2)}) copy-start(f32[1,2,1024]{2,0,1:T(1,128)} %copy-done.43) | copy-start | bytes 24580
  508.3 42.0 %copy-start.46 = (f32[1,2,1024]{2,0,1:T(1,128)S(1)}, f32[1,2,1024]{2,0,1:T(1,128)}, u32[]{:S(2)}) copy-start(f32[1,2,1024]{2,0,1:T(1,128)} %copy-done.45) | copy-start | bytes 24580
  508.3 42.0 %copy-start.48 = (f32[1,2,1024]{2,0,1:T(1,128)S(1)}, f32[1,2,1024]{2,0,1:T(1,128)}, u32[]{:S(2)}) copy-start(f32[1,2,1024]{2,0,1:T(1,128)} %copy-done.47) | copy-start | bytes 24580
  508.3 42.0 %copy-start.50 = (f32[1,2,1024]{2,0,1:T(1,128)S(1)}, f32[1,2,1024]{2,0,1:T(1,128)}, u32[]{:S(2)}) copy-start(f32[1,2,1024]{2,0,1:T(1,128)} %copy-done.49) | copy-start | bytes 24580
  624.4 224.6 %reduce-scatter.9.cloned.1.call-start = ((), (), s32[]{:S(2)}) async-start(), calls=%async_computation.9 | async-start | bytes 8912896 | tf_op jit(solution)/shard_map/reduce_scatter | solution.py:524
  625.0 246.3 %reduce-scatter.17.cloned.1.call-start = ((), (), s32[]{:S(2)}) async-start(), calls=%async_computation.13 | async-start | bytes 1572864 | tf_op jit(solution)/shard_map/reduce_scatter | solution.py:651
  641.1 133.6 %collective-permute-start.1 = (bf16[2048,512]{1,0:T(8,128)(2,1)}, bf16[2048,512]{1,0:T(8,128)(2,1)}, u32[]{:S(2)}, u32[]{:S(2)}) collective-permute-start(bf16[2048,512]{1,0:T(8,128)(2,1)} %constant_dynamic-slice_fusion.3), channel_id=1, source_target_pairs={{0,1},{1,0},{2,3},{3,2},{4,5},{5,4},{6,7},{7,6},{8,9},{9,8},{10,11... | collective-permute-start | bytes 6291464 | tf_op jit(solution)/shard_map/ppermute | solution.py:508
  688.3 91.7 %collective-permute-start.3 = (bf16[2048,512]{1,0:T(8,128)(2,1)}, bf16[2048,512]{1,0:T(8,128)(2,1)}, u32[]{:S(2)}, u32[]{:S(2)}) collective-permute-start(bf16[2048,512]{1,0:T(8,128)(2,1)} %constant_dynamic-slice_fusion.1), channel_id=1, source_target_pairs={{0,1},{1,0},{2,3},{3,2},{4,5},{5,4},{6,7},{7,6},{8,9},{9,8},{10,11... | collective-permute-start | bytes 6291464 | tf_op jit(solution)/shard_map/ppermute | solution.py:508
  692.3 203.3 %reduce-scatter.15.cloned.1.call-start = ((), (), s32[]{:S(2)}) async-start(), calls=%async_computation.12 | async-start | bytes 1794048 | tf_op jit(solution)/shard_map/reduce_scatter | solution.py:529
  774.7 138.3 %reduce-scatter.11.cloned.1.call-start = ((), (), s32[]{:S(2)}) async-start(), calls=%async_computation.10 | async-start | bytes 786432 | tf_op jit(solution)/shard_map/reduce_scatter | solution.py:529
  (76 other events, 754.2 us)
Sparse Core Ops, SparseCore 0:
  17.7 56.2 all-gather.6
  76.8 49.0 all-gather.8
  128.1 49.0 all-gather.10
  491.2 105.1 reduce-scatter.18
  624.5 116.1 reduce-scatter.12
  744.5 104.3 reduce-scatter.8
  851.2 20.0 reduce-scatter.16
  873.6 21.9 reduce-scatter.14
  898.4 14.5 reduce-scatter.10

commit v2 on v1

--- a/solution.py
+++ b/solution.py
@@ -294,7 +294,19 @@
     return jnp.concatenate([jnp.where(lane_low, block, zero), jnp.where(lane_low, zero, block)], axis=0)
 
 
-def scan_forward(per_seq, x_ref, b_ref, c_ref, bt_ref, acol_ref, dtcol_ref, arow_ref, skip_ref, y_ref, st_ref, state, scores):
+def shifts(before, raw):
+    longer = jnp.concatenate([before, raw], axis=0)
+    return [longer[5 + tap : 5 + tap + CHUNK] for tap in range(4)]
+
+
+def convolved(shifted, taps_ref, bias_ref):
+    total = bias_ref[...] + taps_ref[0:1, :] * shifted[0]
+    for tap in range(1, 4):
+        total = total + taps_ref[tap : tap + 1, :] * shifted[tap]
+    return total
+
+
+def scan_forward(per_seq, raw_ref, taps_ref, bias_ref, b_ref, c_ref, bt_ref, acol_ref, dtcol_ref, arow_ref, skip_ref, x_ref, y_ref, st_ref, state, scores, tails):
     step, quad = pl.program_id(0), pl.program_id(1)
     row = lax.broadcasted_iota(jnp.int32, (CHUNK, CHUNK), 0)
     col = lax.broadcasted_iota(jnp.int32, (CHUNK, CHUNK), 1)
@@ -303,11 +315,16 @@
     @pl.when(lax.rem(step, per_seq) == 0)
     def _():
         state[quad] = jnp.zeros((CHUNK, WIDE), F32)
+        tails[quad] = jnp.zeros((8, WIDE), F32)
 
     @pl.when(quad == 0)
     def _():
         scores[...] = jnp.where(row >= col, nt(c_ref[...], b_ref[...]), 0.0)
 
+    raw = raw_ref[...]
+    pre = convolved(shifts(tails[quad], raw), taps_ref, bias_ref)
+    tails[quad] = raw[CHUNK - 8 :]
+    x_ref[...] = (pre * jax.nn.sigmoid(pre)).astype(BF16)
     entering = state[quad]
     st_ref[0] = entering
     across = nn(twice(c_ref[...]), stacked(parts(entering)))
@@ -331,8 +348,8 @@
     state[quad] = jnp.concatenate(ends, axis=1) * entering + added
 
 
-def scan_backward(per_seq, quads, x_ref, dy_ref, b_ref, c_ref, ct_ref, acol_ref, dtcol_ref, arow_ref, skip_ref, st_ref, pick_ref,
-                  dx_ref, db_ref, dc_ref, small_ref, dskip_ref, grads, scores, scores_t, dscores):
+def scan_backward(per_seq, quads, x_ref, raw_ref, before_ref, taps_ref, bias_ref, dy_ref, b_ref, c_ref, ct_ref, acol_ref, dtcol_ref, arow_ref, skip_ref, st_ref, pick_ref,
+                  dx_ref, db_ref, dc_ref, small_ref, dskip_ref, dconv_ref, grads, scores, scores_t, dscores, heads):
     step, quad = pl.program_id(0), pl.program_id(1)
     row = lax.broadcasted_iota(jnp.int32, (CHUNK, CHUNK), 0)
     col = lax.broadcasted_iota(jnp.int32, (CHUNK, CHUNK), 1)
@@ -341,6 +358,7 @@
     @pl.when(lax.rem(step, per_seq) == 0)
     def _():
         grads[quad] = jnp.zeros((CHUNK, WIDE), F32)
+        heads[quad] = jnp.zeros((8, WIDE), F32)
 
     @pl.when(quad == 0)
     def _():
@@ -359,7 +377,7 @@
     kept = jnp.sum(leaving * entering, axis=0, keepdims=True)
     within, within_t = scores[...], scores_t[...]
     dwithin = jnp.zeros((CHUNK, CHUNK), F32)
-    ends, rights, reads, his, los, steps = [], [], [], [], [], []
+    ends, rights, reads, his, los, steps, dxs = [], [], [], [], [], [], []
     for pair in range(QUAD // 2):
         lanes = slice(128 * pair, 128 * pair + 128)
         x = x_ref[:, lanes].astype(F32)
@@ -389,7 +407,7 @@
         out_of = jnp.exp(last - asel)
         du_state = out_of * from_state[:, lanes]
         du_all = du + du_state
-        dx_ref[:, lanes] = dsel * du_all + skip_ref[:, lanes] * dy
+        dxs.append(dsel * du_all + skip_ref[:, lanes] * dy)
         passed = u * du_state
         final = jnp.sum(passed, axis=0, keepdims=True) + last_decay * kept[:, lanes]
         read = dy * into
@@ -403,6 +421,20 @@
         rights.append(out_of * u)
         ends.append(last_decay)
         dskip_ref[0, :, lanes] = jnp.sum((dy * x).reshape(CHUNK // 8, 8, 128), axis=0)
+    before = jnp.where(lax.rem(step + 1, per_seq) == 0, 0.0, before_ref[...])
+    shifted = shifts(before, raw_ref[...])
+    pre = convolved(shifted, taps_ref, bias_ref)
+    sig = jax.nn.sigmoid(pre)
+    dpre = jnp.concatenate(dxs, axis=1) * (sig * (1.0 + pre * (1.0 - sig)))
+    longer = jnp.concatenate([dpre, heads[quad]], axis=0)
+    heads[quad] = dpre[:8]
+    draw = taps_ref[3:4, :] * dpre
+    for tap in range(3):
+        draw = draw + taps_ref[tap : tap + 1, :] * longer[3 - tap : 3 - tap + CHUNK]
+    dx_ref[...] = draw.astype(BF16)
+    for tap in range(4):
+        dconv_ref[0, 8 * tap : 8 * tap + 8, :] = jnp.sum((dpre * shifted[tap]).reshape(CHUNK // 8, 8, WIDE), axis=0)
+    dconv_ref[0, 32:40, :] = jnp.sum(dpre.reshape(CHUNK // 8, 8, WIDE), axis=0)
     read = parts(jnp.concatenate(reads, axis=1))
     right = parts(jnp.concatenate(rights, axis=1))
     dscores[...] += dwithin
@@ -427,28 +459,29 @@
     return maps[:, :half], maps[:, half:], columns(log_decay), columns(step_size), rows
 
 
-def run_forward(values, maps, log_decay, step_size, skip_lanes):
-    tokens, inner = values.shape
+def run_forward(raw, taps, bias, maps, log_decay, step_size, skip_lanes):
+    tokens, inner = raw.shape
     quads, chunks = inner // WIDE, tokens // CHUNK
     enter, read, acol, dtcol, arow = scan_inputs(maps, log_decay, step_size)
+    lane = lambda height: pl.BlockSpec((height, WIDE), lambda i, q: (0, q))
     tall = lambda: pl.BlockSpec((CHUNK, WIDE), lambda i, q: (i, q))
     thin = lambda: pl.BlockSpec((CHUNK, CHUNK), lambda i, q: (i, 0))
     cols = lambda: pl.BlockSpec((1, CHUNK, QUAD), lambda i, q: (q, i, 0))
     return pl.pallas_call(
         partial(scan_forward, SEQ // CHUNK),
         grid=(chunks, quads),
-        in_specs=[tall(), thin(), thin(), pl.BlockSpec((CHUNK, CHUNK), lambda i, q: (0, i)), cols(), cols(),
+        in_specs=[tall(), lane(4), lane(1), thin(), thin(), pl.BlockSpec((CHUNK, CHUNK), lambda i, q: (0, i)), cols(), cols(),
                   pl.BlockSpec((1, QUAD, CHUNK), lambda i, q: (q, 0, i)), pl.BlockSpec((1, WIDE), lambda i, q: (0, q))],
-        out_specs=[tall(), pl.BlockSpec((1, CHUNK, WIDE), lambda i, q: (i, 0, q))],
-        out_shape=[jax.ShapeDtypeStruct((tokens, inner), F32), jax.ShapeDtypeStruct((chunks, CHUNK, inner), F32)],
-        scratch_shapes=[pltpu.VMEM((quads, CHUNK, WIDE), F32), pltpu.VMEM((CHUNK, CHUNK), F32)],
+        out_specs=[tall(), tall(), pl.BlockSpec((1, CHUNK, WIDE), lambda i, q: (i, 0, q))],
+        out_shape=[jax.ShapeDtypeStruct((tokens, inner), BF16), jax.ShapeDtypeStruct((tokens, inner), F32), jax.ShapeDtypeStruct((chunks, CHUNK, inner), F32)],
+        scratch_shapes=[pltpu.VMEM((quads, CHUNK, WIDE), F32), pltpu.VMEM((CHUNK, CHUNK), F32), pltpu.VMEM((quads, 8, WIDE), F32)],
         compiler_params=pltpu.CompilerParams(vmem_limit_bytes=32 * 2**20),
         cost_estimate=pl.CostEstimate(flops=tokens * inner * 1024, bytes_accessed=tokens * inner * 10, transcendentals=tokens * inner * 4),
         name="scan_forward",
-    )(values, enter, read, enter.T, acol, dtcol, arow, skip_lanes)
-
-
-def run_backward(values, dmixed, maps, log_decay, step_size, skip_lanes, states):
+    )(raw, taps, bias[None, :], enter, read, enter.T, acol, dtcol, arow, skip_lanes)
+
+
+def run_backward(values, raw, taps, bias, dmixed, maps, log_decay, step_size, skip_lanes, states):
     tokens, inner = values.shape
     quads, chunks = inner // WIDE, tokens // CHUNK
     enter, read, acol, dtcol, arow = scan_inputs(maps, log_decay, step_size)
@@ -459,27 +492,31 @@
     tall = lambda: pl.BlockSpec((CHUNK, WIDE), lambda i, q: (end - i, q))
     thin = lambda: pl.BlockSpec((CHUNK, CHUNK), lambda i, q: (end - i, 0))
     cols = lambda: pl.BlockSpec((1, CHUNK, QUAD), lambda i, q: (q, end - i, 0))
-    dx, db, dc, small, dskip = pl.pallas_call(
+    lane = lambda height: pl.BlockSpec((height, WIDE), lambda i, q: (0, q))
+    before = pl.BlockSpec((8, WIDE), lambda i, q: (jnp.maximum((end - i) * (CHUNK // 8) - 1, 0), q))
+    dx, db, dc, small, dskip, dconv = pl.pallas_call(
         partial(scan_backward, SEQ // CHUNK, quads),
         grid=(chunks, quads),
-        in_specs=[tall(), tall(), thin(), thin(), pl.BlockSpec((CHUNK, CHUNK), lambda i, q: (0, end - i)), cols(), cols(),
+        in_specs=[tall(), tall(), before, lane(4), lane(1), tall(), thin(), thin(), pl.BlockSpec((CHUNK, CHUNK), lambda i, q: (0, end - i)), cols(), cols(),
                   pl.BlockSpec((1, QUAD, CHUNK), lambda i, q: (q, 0, end - i)), pl.BlockSpec((1, WIDE), lambda i, q: (0, q)),
                   pl.BlockSpec((1, CHUNK, WIDE), lambda i, q: (end - i, 0, q)), pl.BlockSpec((3 * WIDE, 128), lambda i, q: (0, 0))],
         out_specs=[tall(), thin(), thin(), pl.BlockSpec((1, CHUNK, 128), lambda i, q: (q, end - i, 0)),
-                   pl.BlockSpec((1, 8, WIDE), lambda i, q: (end - i, 0, q))],
-        out_shape=[jax.ShapeDtypeStruct((tokens, inner), F32), jax.ShapeDtypeStruct((tokens, CHUNK), F32),
+                   pl.BlockSpec((1, 8, WIDE), lambda i, q: (end - i, 0, q)),
+                   pl.BlockSpec((1, 40, WIDE), lambda i, q: (end - i, 0, q))],
+        out_shape=[jax.ShapeDtypeStruct((tokens, inner), BF16), jax.ShapeDtypeStruct((tokens, CHUNK), F32),
                    jax.ShapeDtypeStruct((tokens, CHUNK), F32), jax.ShapeDtypeStruct((quads, tokens, 128), F32),
-                   jax.ShapeDtypeStruct((chunks, 8, inner), F32)],
-        scratch_shapes=[pltpu.VMEM((quads, CHUNK, WIDE), F32)] + [pltpu.VMEM((CHUNK, CHUNK), F32)] * 3,
+                   jax.ShapeDtypeStruct((chunks, 8, inner), F32), jax.ShapeDtypeStruct((chunks, 40, inner), F32)],
+        scratch_shapes=[pltpu.VMEM((quads, CHUNK, WIDE), F32)] + [pltpu.VMEM((CHUNK, CHUNK), F32)] * 3 + [pltpu.VMEM((quads, 8, WIDE), F32)],
         compiler_params=pltpu.CompilerParams(vmem_limit_bytes=32 * 2**20),
         cost_estimate=pl.CostEstimate(flops=tokens * inner * 2560, bytes_accessed=tokens * inner * 12, transcendentals=tokens * inner * 8),
         name="scan_backward",
-    )(values, dmixed, enter, read, read.T, acol, dtcol, arow, skip_lanes, states, picks)
+    )(values, raw, raw, taps, bias[None, :], dmixed, enter, read, read.T, acol, dtcol, arow, skip_lanes, states, picks)
     per_head = lambda part: part.transpose(1, 0, 2).reshape(tokens, quads * QUAD)
     dlog = per_head(small[:, :, :QUAD])
     dstep = per_head(small[:, :, QUAD : 2 * QUAD])
     dskip = jnp.sum(dskip.reshape(chunks * 8, inner // HEADDIM, HEADDIM), axis=(0, 2))
-    return dx, jnp.concatenate([db, dc], axis=1), dlog, dstep, dskip
+    dconv = jnp.sum(dconv.reshape(chunks, 5, 8, inner), axis=(0, 2))
+    return dx, jnp.concatenate([db, dc], axis=1), dlog, dstep, dskip, dconv
 
 
 def chunk_sums(v, lower):
@@ -510,9 +547,8 @@
     return jnp.concatenate([jnp.where(first, mine, came), jnp.where(first, came, mine)], axis=0)
 
 
-def gather_columns(shards):
+def gather_columns(shards, wide):
     widths = [shard.shape[1] for shard in shards]
-    wide = lax.all_gather(jnp.concatenate(shards, axis=1), "tp", axis=0)
     pieces, at = [], 0
     for width in widths:
         pieces += [wide[part, :, at : at + width] for part in range(wide.shape[0])]
@@ -520,18 +556,16 @@
     return lax.all_gather(jnp.concatenate(pieces, axis=1), "dp", axis=0, tiled=True)
 
 
-def scatter_columns(whole, widths, tp):
-    rows = lax.psum_scatter(whole, "dp", scatter_dimension=0, tiled=True)
-    pieces, at = [], 0
-    for width in widths:
-        pieces.append(rows[:, at : at + width * tp].reshape(rows.shape[0], tp, width))
-        at += width * tp
-    mine = lax.psum_scatter(jnp.concatenate(pieces, axis=2).transpose(1, 0, 2), "tp", scatter_dimension=0, tiled=True)[0]
-    outs, at = [], 0
-    for width in widths:
-        outs.append(mine[:, at : at + width])
-        at += width
-    return outs
+def sum_half(whole, axis):
+    me = lax.axis_index("tp")
+    size = whole.shape[axis] // 2
+    mine = lax.dynamic_slice_in_dim(whole, me * size, size, axis)
+    other = lax.dynamic_slice_in_dim(whole, (1 - me) * size, size, axis).astype(BF16)
+    return mine + lax.ppermute(other, "tp", [(0, 1), (1, 0)]).astype(F32)
+
+
+def sum_rows(halves):
+    return lax.psum_scatter(halves, "dp", scatter_dimension=0, tiled=True)
 
 
 def by_sequences(
@@ -560,12 +594,17 @@
         piece = packed[:, at : at + v.size].reshape((tp,) + v.shape)
         at += v.size
         fulls.append(piece.reshape(-1) if v.ndim == 1 else piece.transpose(1, 0, 2).reshape(v.shape[0], -1))
+    low_parts = [proj_value, proj_state, proj_step]
+    low_wide = lax.all_gather(jnp.concatenate(low_parts, axis=1), "tp", axis=0)
+    gate_wide = lax.all_gather(proj_gate, "tp", axis=0)
+    out_rows = lax.all_gather(proj_out, "tp", axis=0, tiled=True)
+    resid_in, cotangent, low_wide, gate_wide, out_rows, fulls = lax.optimization_barrier(
+        (resid_in, cotangent, low_wide, gate_wide, out_rows, fulls)
+    )
     gain, conv_v, bias_v, conv_s, bias_s, bias_step, log_rate, skip, gain_out = fulls
-
     resid = to_sequences(resid_in).astype(F32)
-    low_w = gather_columns([proj_value, proj_state, proj_step])
-    gate_w = gather_columns([proj_gate])
-    out_rows = lax.all_gather(proj_out, "tp", axis=0, tiled=True)
+    low_w = gather_columns(low_parts, low_wide)
+    gate_w = gather_columns([proj_gate], gate_wide)
     out_w = lax.all_gather(out_rows, "dp", axis=1, tiled=True)
     cot_low = to_sequences(cotangent)
 
@@ -587,15 +626,13 @@
         convolved = jax.vmap(causal_conv, (0, None, None))(framed, kernel, kernel_bias)
         return jax.nn.silu(convolved).reshape(raw.shape)
 
-    value_act, value_pull = jax.vjp(conv_act, value_raw, conv_v, bias_v)
-    values = value_act.astype(BF16)
     state_act, state_pull = jax.vjp(conv_act, state_raw, conv_s, bias_s)
     maps = state_act.astype(BF16)
     step_size, step_pull = jax.vjp(lambda v: jax.nn.softplus(v + bias_step), step_raw)
     rate = -jnp.exp(log_rate)
     log_decay = chunk_sums(step_size * rate, True)
     skip_lanes = jnp.repeat(skip, HEADDIM)[None, :]
-    mixed, entering = run_forward(values, maps, log_decay, step_size, skip_lanes)
+    values, mixed, entering = run_forward(value_raw, conv_v, bias_v, maps, log_decay, step_size, skip_lanes)
 
     gate_raw = product(normed_in, gate_w)
     gated, gate_pull = jax.vjp(gating, mixed, gate_raw)
@@ -605,7 +642,7 @@
     normed_out = (scaled * gain_out).astype(BF16)
     block_out = to_features((resid + product(normed_out, out_w)).astype(BF16))
     normed_grad = product_right(cot_low, out_w)
-    out_grad = product_left(normed_out, cot_low)
+    out_grad = product_left(cot_low, normed_out)
     gate_gain_grad = jnp.sum(normed_grad * scaled, axis=0)
     weighted = normed_grad * gain_out
     crossed = jnp.sum(weighted * gated, axis=-1, keepdims=True)
@@ -614,21 +651,29 @@
     mixed_grad, gate_raw_grad = gate_pull(gated_grad)
     gate_low = gate_raw_grad.astype(BF16)
     gate_w_grad = product_left(normed_in, gate_low)
-    mixed_grad, gate_w_grad, out_grad = lax.optimization_barrier((mixed_grad, gate_w_grad, out_grad))
-
-    values_grad, maps_grad, dlog, dstep, skip_grad = run_backward(
-        values, mixed_grad, maps, log_decay, step_size, skip_lanes, entering
-    )
+    early_half = jnp.concatenate([sum_half(gate_w_grad, 1), sum_half(out_grad, 1)], axis=1)
+    mixed_grad, early_half = lax.optimization_barrier((mixed_grad, early_half))
+    early_mine = sum_rows(early_half)
+
+    value_low, maps_grad, dlog, dstep, skip_grad, conv_grads = run_backward(
+        values, value_raw, conv_v, bias_v, mixed_grad, maps, log_decay, step_size, skip_lanes, entering
+    )
+    value_low, early_mine = lax.optimization_barrier((value_low, early_mine))
+    gate_mine, out_mine = early_mine[:, : inner // 2], early_mine[:, inner // 2 :].T
     summed = chunk_sums(dlog, False)
     decay_grad = rate * jnp.sum(summed * step_size, axis=0)
     (step_grad,) = step_pull(dstep + summed * rate)
     step_bias_grad = jnp.sum(step_grad, axis=0)
-    value_raw_grad, conv_value_grad, value_bias_grad = value_pull(values_grad)
+    conv_value_grad, value_bias_grad = conv_grads[:4], conv_grads[4]
     state_raw_grad, conv_state_grad, state_bias_grad = state_pull(maps_grad)
     rest_low = jnp.concatenate([state_raw_grad.astype(BF16), step_grad.astype(BF16)], axis=1)
-    value_low = value_raw_grad.astype(BF16)
     value_w_grad = product_left(normed_in, value_low)
     rest_w_grad = product_left(normed_in, rest_low)
+    low_half = [sum_half(v, 1) for v in (value_w_grad, rest_w_grad[:, :states], rest_w_grad[:, states:])]
+    low_mine = sum_rows(jnp.concatenate(low_half, axis=1))
+    value_mine = low_mine[:, : inner // 2]
+    state_mine = low_mine[:, inner // 2 : (inner + states) // 2]
+    step_mine = low_mine[:, (inner + states) // 2 :]
     input_grad = (
         product_right(gate_low, gate_w) + product_right(value_low, value_w) + product_right(rest_low, rest_w)
     )
@@ -640,15 +685,6 @@
         cot_low.astype(F32) + pulled * inv_rms - resid * rms_cubed * (crossed_rows / resid.shape[1])
     ).astype(BF16)
     grad_in = to_features(grad_in)
-
-    (gate_mine,) = scatter_columns(gate_w_grad, [proj_gate.shape[1]], tp)
-    value_mine, state_mine, step_mine = scatter_columns(
-        jnp.concatenate([value_w_grad, rest_w_grad], axis=1),
-        [proj_value.shape[1], proj_state.shape[1], proj_step.shape[1]],
-        tp,
-    )
-    out_cols = lax.psum_scatter(out_grad, "dp", scatter_dimension=1, tiled=True)
-    out_mine = lax.psum_scatter(out_cols, "tp", scatter_dimension=0, tiled=True)
 
     small_out = [gain_grad, conv_value_grad, value_bias_grad, conv_state_grad, state_bias_grad, step_bias_grad, decay_grad, skip_grad, gate_gain_grad]
     split = [

time: 924 us -> 838 us (0.907)
  other arithmetic: 225 us -> 103 us
  blocking collectives: 185 us -> 96.1 us
  waiting for transfers between devices: 114 us -> 175 us
  Pallas kernels: 136 us -> 191 us
    reduce_scatter x5 -> x2, waiting for transfers between devices: 113 us -> 0.01 us  [sum_rows(): return lax.psum_scatter(halves, 'dp', scatter_dimension=0, tiled=True)]
    ppermute x0 -> x5, waiting for transfers between devices: none -> 97.3 us  [sum_half(): return mine + lax.ppermute(other, 'tp', [(0, 1), (1, 0)]).astype(F32)]
    all_gather x1, blocking collectives: 89.3 us -> 6.66 us  [by_sequences(): out_rows = lax.all_gather(proj_out, 'tp', axis=0, tiled=True)]
    ppermute x2, waiting for transfers between devices: 0.01 us -> 77.5 us  [to_sequences(): came = lax.ppermute(other, 'tp', [(0, 1), (1, 0)])]
    convert_element_type x2 -> x0, other arithmetic: 56.6 us -> none  [the longest x1 33 us: by_sequences(): values = value_act.astype(BF16)]
    reduce_sum x2 -> x1, other arithmetic: 48.6 us -> 6.33 us  [causal_conv(): summed = summed + kernel[offset][None, :] * padded[offset:offset + length]]
    pallas_call x1, Pallas kernels: 88.5 us -> 127 us  [run_backward(): pl.pallas_call(partial(scan_backward, SEQ // CHUNK, quads), grid=(chunks,...]
    mul x2 -> x1, other arithmetic: 31.1 us -> 3.96 us  [causal_conv(): summed = summed + kernel[offset][None, :] * padded[offset:offset + length]]
  transfers between devices with their start and end apart: 13 -> 14, of which waited for: 4 -> 5; matrix products, arithmetic and copies ran while one was open for 37% -> 28% of each run, Pallas kernels for 5% -> 23%
where the time goes in v2:
time: 838 us; the launch traced here: 827 us
  Pallas kernels  191 us (23%)
  waiting for transfers between devices  175 us (21%)
  matrix products  157 us (19%)
  other arithmetic  103 us (12%)
  blocking collectives  96.1 us (11%)
  local copies, waits for them, and re-layouts  78.5 us (9%)
  between operations  15.9 us (2%)
  starting transfers between devices  10.6 us (1%)
    pallas_call x1, Pallas kernels, run_backward(): pl.pallas_call(partial(scan_backward, SEQ // CHUNK, quads), grid=(chunks,...  127 us
    ppermute x5, waiting for transfers between devices, sum_half(): return mine + lax.ppermute(other, 'tp', [(0, 1), (1, 0)]).astype(F32)  97.3 us
    ppermute x2, waiting for transfers between devices, to_sequences(): came = lax.ppermute(other, 'tp', [(0, 1), (1, 0)])  77.5 us
    psum x1, blocking collectives, by_sequences(): sums = lax.psum(jnp.concatenate(split, axis=1), ('dp', 'tp'))  67.3 us
    pallas_call x1, Pallas kernels, run_forward(): pl.pallas_call(partial(scan_forward, SEQ // CHUNK), grid=(chunks, quads),...  64.4 us
    dot_general x4, matrix products, product_right(): jnp.einsum('tc,kc->tk', matrix, factor, preferred_element_type=jnp.float32)  57.4 us
    dot_general x4, matrix products, product(): return jnp.dot(matrix, factor, preferred_element_type=jnp.float32)  57 us
    dot_general x4, matrix products, product_left(): jnp.einsum('tk,tc->kc', matrix, factor, preferred_element_type=jnp.float32)  42.1 us
  transfers between devices with their start and end apart: 14, of which 5 were waited for; matrix products, arithmetic and copies ran while one was open for 28% of the time, Pallas kernels for 23%

profile of v2, /device:TPU:0, one launch (start us, length us, event | category | flops | bytes accessed | tf_op | source)
XLA Modules:
  0.0 827.2 jit_solution(9168413733716854493)
XLA Ops:
  12.0 10.3 %all-reduce.9 = f32[14688]{0:T(1024)S(1)} all-reduce(f32[14688]{0:T(1024)S(1)} %dynamic-update-slice), channel_id=4, replica_groups=mesh['dp'=16,'tp'=2] {'tp'}, use_global_device_ids=true, to_apply=%add.9 | all-reduce | flops 14688 | bytes 117504
  24.6 6.0 all-gather
  30.6 6.7 all_gather.34
  37.2 5.8 all-gather.1
  51.9 45.1 %collective-permute-done = bf16[2048,512]{1,0:T(8,128)(2,1)} collective-permute-done((bf16[2048,512]{1,0:T(8,128)(2,1)}, bf16[2048,512]{1,0:T(8,128)(2,1)}, u32[]{:S(2)}, u32[]{:S(2)}) %collective-permute-start) | collective-permute-done | bytes 2097184 | tf_op jit(solution)/shard_map/ppermute | solution.py:535
  103.0 32.5 %collective-permute-done.2 = bf16[2048,512]{1,0:T(8,128)(2,1)} collective-permute-done((bf16[2048,512]{1,0:T(8,128)(2,1)}, bf16[2048,512]{1,0:T(8,128)(2,1)}, u32[]{:S(2)}, u32[]{:S(2)}) %collective-permute-start.2) | collective-permute-done | bytes 2097184 | tf_op jit(solution)/shard_map/ppermute | solution.py:535
  135.4 4.4 broadcast_select_fusion.3
  139.9 3.8 fusion.29
  150.1 6.9 fusion.26
  157.8 3.5 copy.79
  161.4 15.3 %fusion.17.raw_ref.before_ref = f32[2048,2048]{1,0:T(8,128)} fusion(bf16[1024,2336]{1,0:T(8,128)(2,1)} %all-gather.7.cloned.1.call-done, f32[1024]{0:T(1024)S(1)} %bitcast.180, f32[2048]{0:T(1024)S(1)} %get-tuple-element.182, bf16[2048,512]{1,0:T(8,128)(2,1)} %copy-done.20, bf16[2048,512]{1,0:T(8,128)(2,1)} %copy-done.16), kind=kOutput, calls=%fused_computation.44 | convolution fusion | flops 8604614656 | bytes 25178112 | tf_op jit(solution)/shard_map/dot_general | solution.py:71
  176.7 64.4 %scan_forward.1 = (bf16[2048,2048]{1,0:T(8,128)(2,1)S(1)}, f32[2048,2048]{1,0:T(8,128)}, f32[16,128,2048]{2,1,0:T(8,128)}) custom-call(f32[2048,2048]{1,0:T(8,128)} %fusion.17.raw_ref.before_ref, f32[4,2048]{1,0:T(4,128)S(1)} %bitcast.165, f32[1,2048]{1,0:T(1,128)S(1)} %bitcast.167, bf16[2048,128]{1,0:T(8,128)(2,1)S(1)} %copy.81.b_ref, ...), custom_call_target="tpu_custom_call" | custom-call | flops 4294967296 | bytes 41943040 | tf_op jit(solution)/shard_map/scan_forward/pallas_call | solution.py:470
  244.4 23.2 %multiply_reduce_fusion.2 = (f32[2048]{0:T(1024)S(1)}, f32[2048,2048]{1,0:T(8,128)}, f32[2048,2048]{1,0:T(8,128)}) fusion(f32[2048,2048]{1,0:T(8,128)} %get-tuple-element.53, bf16[1024,2048]{1,0:T(8,128)(2,1)} %all-gather.9.cloned.1.call-done, f32[1024]{0:T(1024)S(1)} %bitcast.181, f32[2048]{0:T(1024)S(1)} %get-tuple-element.182, ...), kind=kOutput, calls=%fused_computation.8 | convolution fusion | flops 8633972736 | bytes 58740736 | tf_op jit(solution)/shard_map/dot_general | solution.py:71
  267.7 18.4 %multiply_reduce_fusion = (f32[2048]{0:T(1024)S(1)}, f32[2048]{0:T(1024)S(1)}, f32[2048,2048]{1,0:T(8,128)}) fusion(f32[2048,2048]{1,0:T(8,128)} %get-tuple-element.131, f32[2048]{0:T(1024)S(1)} %get-tuple-element.184, f32[2048]{0:T(1024)S(1)} %get-tuple-element.55, bf16[2048,1024]{0,1:T(8,128)(2,1)} %all-gather.11.cloned.1.call-done, ...), kind=kOutput, calls=%fused_computation.4 | convolution fusion | flops 8623484928 | bytes 41975808 | tf_op jit(solution)/shard_map/tc,kc->tk/dot_general | solution.py:79
  286.1 32.3 %fusion.14 = (f32[2048,2048]{1,0:T(8,128)}, bf16[2048,2048]{1,0:T(8,128)(2,1)}) fusion(f32[2048]{0:T(1024)S(1)} %broadcast_multiply_fusion.4, f32[2048,2048]{1,0:T(8,128)} %get-tuple-element.131, f32[2048,2048]{1,0:T(8,128)} %get-tuple-element.190, f32[2048]{0:T(1024)S(1)} %get-tuple-element.183, f32[2048]{0:T(1024)S(1)} %get-tuple-element.55, ...), kind=kLoop, calls=%fused_computation.28 | loop fusion | flops 75497472 | bytes 92307456 | tf_op jit(solution)/shard_map/transpose(jvp())/mul | solution.py:83
  318.3 12.1 %fusion.64 = f32[1024,2048]{1,0:T(8,128)S(1)} fusion(bf16[2048,2048]{1,0:T(8,128)(2,1)} %get-tuple-element.135, f32[1024]{0:T(1024)S(1)} %bitcast.182, f32[2048]{0:T(1024)S(1)} %get-tuple-element.182, bf16[2048,512]{1,0:T(8,128)(2,1)S(1)} %copy-done.21, bf16[2048,512]{1,0:T(8,128)(2,1)S(1)} %copy-done.17), kind=kOutput, calls=%fused_computation.181 | convolution fusion | flops 8604614656 | bytes 20983808 | tf_op jit(solution)/shard_map/tk,tc->kc/dot_general | solution.py:75
  336.9 13.4 %fusion.23 = f32[1024,2048]{1,0:T(8,128)S(1)} fusion(bf16[2048,512]{1,0:T(8,128)(2,1)S(1)} %copy-done.27, bf16[2048,512]{1,0:T(8,128)(2,1)S(1)} %copy-done.26, f32[2048,2048]{1,0:T(8,128)} %get-tuple-element.131, f32[2048]{0:T(1024)S(1)} %get-tuple-element.55, f32[2048]{0:T(1024)S(1)} %get-tuple-element.184), kind=kOutput, calls=%fused_computation.74 | convolution fusion | flops 8610906112 | bytes 29376512 | tf_op jit(solution)/shard_map/tk,tc->kc/dot_general | solution.py:75
  355.8 28.4 %collective-permute-done.3 = bf16[1024,1024]{1,0:T(8,128)(2,1)} collective-permute-done((bf16[1024,1024]{1,0:T(8,128)(2,1)}, bf16[1024,1024]{1,0:T(8,128)(2,1)}, u32[]{:S(2)}, u32[]{:S(2)}) %collective-permute-start.3) | collective-permute-done | bytes 2097184 | tf_op jit(solution)/shard_map/ppermute | solution.py:564
  387.7 34.0 %collective-permute-done.4 = bf16[1024,1024]{1,0:T(8,128)(2,1)} collective-permute-done((bf16[1024,1024]{1,0:T(8,128)(2,1)}, bf16[1024,1024]{1,0:T(8,128)(2,1)}, u32[]{:S(2)}, u32[]{:S(2)}) %collective-permute-start.4) | collective-permute-done | bytes 2097184 | tf_op jit(solution)/shard_map/ppermute | solution.py:564
  424.1 3.9 pad_maximum_fusion
  429.0 14.7 %fusion.9 = bf16[2048,1024]{1,0:T(8,128)(2,1)S(1)} fusion(bf16[2048,1024]{0,1:T(8,128)(2,1)} %all-gather.11.cloned.1.call-done, f32[2048,2048]{1,0:T(8,128)} %get-tuple-element.131, f32[2048]{0:T(1024)S(1)} %get-tuple-element.55, f32[2048]{0:T(1024)S(1)} %get-tuple-element.184, bf16[2048,512]{1,0:T(8,128)(2,1)} %copy-done.20, bf16[2048,512]{1,0:T(8,128)(2,1)} %copy-done.16), kind=kOutput, calls=%fused_computation.21 | convolution fusion | flops 8615100416 | bytes 29376512 | tf_op jit(solution)/shard_map/dot_general | solution.py:71
  448.5 14.6 %fusion.79 = f32[2048,1024]{1,0:T(8,128)} fusion(bf16[2048,2048]{1,0:T(8,128)(2,1)} %get-tuple-element.135, bf16[1024,2048]{1,0:T(8,128)(2,1)S(1)} %copy-done.55), kind=kOutput, calls=%fused_computation.189 | convolution fusion | flops 8589934592 | bytes 20971520 | tf_op jit(solution)/shard_map/tc,kc->tk/dot_general | solution.py:79
  463.2 126.9 %scan_backward.1 = (bf16[2048,2048]{1,0:T(8,128)(2,1)}, f32[2048,128]{1,0:T(8,128)S(1)}, f32[2048,128]{1,0:T(8,128)S(1)}, f32[4,2048,128]{2,1,0:T(8,128)S(1)}, f...) custom-call(bf16[2048,2048]{1,0:T(8,128)(2,1)} %copy-done.5, f32[2048,2048]{1,0:T(8,128)} %fusion.17.raw_ref.before_ref, ...), custom_call_target="tpu_custom_call" | custom-call | flops 10737418240 | bytes 50331648 | tf_op jit(solution)/shard_map/scan_backward/pallas_call | solution.py:497
  598.2 8.1 slice_bitcast_fusion.1
  612.5 6.3 multiply_reduce_fusion.5
  618.9 4.0 broadcast_multiply_fusion
  622.9 13.7 %fusion.62 = f32[1024,2048]{1,0:T(8,128)S(1)} fusion(bf16[2048,2048]{1,0:T(8,128)(2,1)} %get-tuple-element.63, f32[1024]{0:T(1024)S(1)} %bitcast.183, f32[2048]{0:T(1024)S(1)} %get-tuple-element.182, bf16[2048,512]{1,0:T(8,128)(2,1)} %copy-done.20, bf16[2048,512]{1,0:T(8,128)(2,1)} %copy-done.16), kind=kOutput, calls=%fused_computation.180 | convolution fusion | flops 8604614656 | bytes 20983808 | tf_op jit(solution)/shard_map/tk,tc->kc/dot_general | solution.py:75
  655.4 34.9 %collective-permute-done.8 = bf16[1024,16]{1,0:T(8,128)(2,1)} collective-permute-done((bf16[1024,16]{1,0:T(8,128)(2,1)}, bf16[1024,16]{1,0:T(8,128)(2,1)}, u32[]{:S(2)}, u32[]{:S(2)}) %collective-permute-start.8) | collective-permute-done | bytes 32800 | tf_op jit(solution)/shard_map/ppermute | solution.py:564
  699.0 14.7 %fusion.15 = f32[2048,1024]{1,0:T(8,128)} fusion(bf16[2048,2048]{1,0:T(8,128)(2,1)} %get-tuple-element.63, bf16[1024,2336]{1,0:T(8,128)(2,1)} %all-gather.7.cloned.1.call-done), kind=kOutput, calls=%fused_computation.42 | convolution fusion | flops 8589934592 | bytes 20971520 | tf_op jit(solution)/shard_map/tc,kc->tk/dot_general | solution.py:79
  713.7 9.7 %fusion.7 = (f32[1024]{0:T(1024)S(1)}, f32[2048]{0:T(1024)S(1)}, f32[2048,1024]{1,0:T(8,128)S(1)}) fusion(f32[2048]{0:T(1024)S(1)} %get-tuple-element.182, bf16[2048,512]{1,0:T(8,128)(2,1)S(1)} %copy-done.23, bf16[2048,512]{1,0:T(8,128)(2,1)S(1)} %copy-done.19, f32[1024]{0:T(1024)S(1)} %bitcast.185, bf16[1024,2336]{1,0:T(8,128)(2,1)} %all-gather.7.cloned.1.call-done, ...), kind=kOutput, calls=%fused_computation.19 | convolution fusion | flops 1235481600 | bytes 31350784 | tf_op jit(solution)/shard_map/tc,kc->tk/dot_general | solution.py:79
  723.4 4.7 fusion.12
  739.1 67.3 %psum.7 = f32[2,7344]{1,0:T(2,128)S(1)} all-reduce(f32[2,7344]{1,0:T(2,128)S(1)} %concatenate.57), channel_id=1, replica_groups=mesh['dp'=16,'tp'=2] {'dp','tp'}, use_global_device_ids=true, to_apply=%region_18.19 | all-reduce | flops 14688 | bytes 117504 | tf_op jit(solution)/shard_map/psum | solution.py:694
  (253 shorter events, 121.4 us)
Async XLA Ops:
  7.2 132.7 %all-gather.7.cloned.1.call-start = ((), (), s32[]{:S(2)}) async-start(), calls=%async_computation.2 | async-start | bytes 5292032 | tf_op jit(solution)/shard_map/all_gather | solution.py:556
  22.6 122.7 %copy-start.51 = (f32[32]{0:T(128)}, f32[32]{0:T(128)S(1)}, u32[]{:S(2)}) copy-start(f32[32]{0:T(128)S(1)} %reshape.290) | copy-start | bytes 388
  22.7 29.1 %copy-start.56 = (f32[32]{0:T(128)}, f32[32]{0:T(128)S(1)}, u32[]{:S(2)}) copy-start(f32[32]{0:T(128)S(1)} %reshape.291) | copy-start | bytes 388
  22.8 153.8 %copy-start.10 = (f32[1,4,2,1024]{3,1,2,0:T(4,128)}, f32[1,4,2,1024]{3,1,2,0:T(4,128)S(1)}, u32[]{:S(2)}) copy-start(f32[1,4,2,1024]{3,1,2,0:T(4,128)S(1)} %copy.104) | copy-start | bytes 98308
  43.1 133.6 %copy-start.14 = (f32[2048]{0:T(1024)}, f32[2048]{0:T(1024)S(1)}, u32[]{:S(2)}) copy-start(f32[2048]{0:T(1024)S(1)} %get-tuple-element.47) | copy-start | bytes 24580
  44.0 200.4 %all-gather.9.cloned.1.call-start = ((), (), s32[]{:S(2)}) async-start(), calls=%async_computation.3 | async-start | bytes 4456448 | tf_op jit(solution)/shard_map/all_gather | solution.py:556
  44.8 222.8 %all-gather.11.cloned.1.call-start = ((), (), s32[]{:S(2)}) async-start(), calls=%async_computation.4 | async-start | bytes 4456448 | tf_op jit(solution)/shard_map/all_gather | solution.py:608
  48.1 48.9 %collective-permute-start = (bf16[2048,512]{1,0:T(8,128)(2,1)}, bf16[2048,512]{1,0:T(8,128)(2,1)}, u32[]{:S(2)}, u32[]{:S(2)}) collective-permute-start(bf16[2048,512]{1,0:T(8,128)(2,1)} %constant_dynamic-slice_fusion.4), channel_id=1, source_target_pairs={{0,1},{1,0},{2,3},{3,2},{4,5},{5,4},{6,7},{7,6},{8,9},{9,8},{10,11... | collective-permute-start | bytes 6291464 | tf_op jit(solution)/shard_map/ppermute | solution.py:535
  51.2 84.2 %collective-permute-start.2 = (bf16[2048,512]{1,0:T(8,128)(2,1)}, bf16[2048,512]{1,0:T(8,128)(2,1)}, u32[]{:S(2)}, u32[]{:S(2)}) collective-permute-start(bf16[2048,512]{1,0:T(8,128)(2,1)} %constant_dynamic-slice_fusion.2), channel_id=1, source_target_pairs={{0,1},{1,0},{2,3},{3,2},{4,5},{5,4},{6,7},{7,6},{8,9},{9,8},{10,11... | collective-permute-start | bytes 6291464 | tf_op jit(solution)/shard_map/ppermute | solution.py:535
  51.6 571.3 %reduce-scatter.3.cloned.1.call-start = ((), (), s32[]{:S(2)}) async-start(), calls=%async_computation.5 | async-start | bytes 8912896 | tf_op jit(solution)/shard_map/reduce_scatter | solution.py:568
  51.8 124.9 %copy-start.12 = (f32[1,2048]{1,0:T(1,128)}, f32[1,2048]{1,0:T(1,128)S(1)}, u32[]{:S(2)}) copy-start(f32[1,2048]{1,0:T(1,128)S(1)} %broadcast_in_dim_reshape.3.skip_ref) | copy-start | bytes 24580
  51.8 93.5 %copy-start.53 = (f32[32]{0:T(128)}, f32[32]{0:T(128)S(1)}, u32[]{:S(2)}) copy-start(f32[32]{0:T(128)S(1)} %exponential_negate_fusion) | copy-start | bytes 388
  51.9 98.2 %copy-start.43 = (f32[1,256]{1,0:T(1,128)}, f32[1,256]{1,0:T(1,128)S(1)}, u32[]{:S(2)}) copy-start(f32[1,256]{1,0:T(1,128)S(1)} %get-tuple-element.185) | copy-start | bytes 3076
  51.9 98.2 %copy-start.45 = (f32[1,256]{1,0:T(1,128)}, f32[1,256]{1,0:T(1,128)S(1)}, u32[]{:S(2)}) copy-start(f32[1,256]{1,0:T(1,128)S(1)} %get-tuple-element.186) | copy-start | bytes 3076
  51.9 98.2 %copy-start.47 = (f32[1,256]{1,0:T(1,128)}, f32[1,256]{1,0:T(1,128)S(1)}, u32[]{:S(2)}) copy-start(f32[1,256]{1,0:T(1,128)S(1)} %get-tuple-element.187) | copy-start | bytes 3076
  51.9 98.2 %copy-start.49 = (f32[1,256]{1,0:T(1,128)}, f32[1,256]{1,0:T(1,128)S(1)}, u32[]{:S(2)}) copy-start(f32[1,256]{1,0:T(1,128)S(1)} %get-tuple-element.188) | copy-start | bytes 3076
  100.1 35.4 %copy-start.37 = (bf16[4096,512]{1,0:T(8,128)(2,1)S(1)}, bf16[4096,512]{1,0:T(8,128)(2,1)}, u32[]{:S(2)}) copy-start(bf16[4096,512]{1,0:T(8,128)(2,1)} %param.31) | copy-start | bytes 12582916
  286.0 32.3 %copy-start.17 = (bf16[2048,512]{1,0:T(8,128)(2,1)S(1)}, bf16[2048,512]{1,0:T(8,128)(2,1)}, u32[]{:S(2)}) copy-start(bf16[2048,512]{1,0:T(8,128)(2,1)} %copy-done.16) | copy-start | bytes 6291460
  286.0 32.3 %copy-start.21 = (bf16[2048,512]{1,0:T(8,128)(2,1)S(1)}, bf16[2048,512]{1,0:T(8,128)(2,1)}, u32[]{:S(2)}) copy-start(bf16[2048,512]{1,0:T(8,128)(2,1)} %copy-done.20) | copy-start | bytes 6291460
  335.4 48.9 %collective-permute-start.3 = (bf16[1024,1024]{1,0:T(8,128)(2,1)}, bf16[1024,1024]{1,0:T(8,128)(2,1)}, u32[]{:S(2)}, u32[]{:S(2)}) collective-permute-start(bf16[1024,1024]{1,0:T(8,128)(2,1)} %dynamic-slice_convert_fusion.2), channel_id=1, source_target_pairs={{0,1},{1,0},{2,3},{3,2},{4,5},{5,4},{6,7},{7,6},{8,9},{9,8},{10,11... | collective-permute-start | bytes 6291464 | tf_op jit(solution)/shard_map/ppermute | solution.py:564
  355.3 66.4 %collective-permute-start.4 = (bf16[1024,1024]{1,0:T(8,128)(2,1)}, bf16[1024,1024]{1,0:T(8,128)(2,1)}, u32[]{:S(2)}, u32[]{:S(2)}) collective-permute-start(bf16[1024,1024]{1,0:T(8,128)(2,1)} %dynamic-slice_convert_fusion.1), channel_id=1, source_target_pairs={{0,1},{1,0},{2,3},{3,2},{4,5},{5,4},{6,7},{7,6},{8,9},{9,8},{10,11... | collective-permute-start | bytes 6291464 | tf_op jit(solution)/shard_map/ppermute | solution.py:564
  355.8 66.0 %copy-start.34 = (f32[1024,2048]{1,0:T(8,128)S(1)}, f32[1024,2048]{1,0:T(8,128)}, u32[]{:S(2)}) copy-start(f32[1024,2048]{1,0:T(8,128)} %copy-done.33) | copy-start | bytes 25165828
  428.0 387.7 %reduce-scatter.5.cloned.1.call-start = ((), (), s32[]{:S(2)}) async-start(), calls=%async_computation.6 | async-start | bytes 5570560 | tf_op jit(solution)/shard_map/reduce_scatter | solution.py:568
  443.7 19.4 %copy-start.38 = (bf16[2048,1024]{1,0:T(8,128)(2,1)}, bf16[2048,1024]{1,0:T(8,128)(2,1)S(1)}, u32[]{:S(2)}) copy-start(bf16[2048,1024]{1,0:T(8,128)(2,1)S(1)} %fusion.9) | copy-start | bytes 12582916
  445.4 288.2 %collective-permute-start.1 = (bf16[2048,512]{1,0:T(8,128)(2,1)}, bf16[2048,512]{1,0:T(8,128)(2,1)}, u32[]{:S(2)}, u32[]{:S(2)}) collective-permute-start(bf16[2048,512]{1,0:T(8,128)(2,1)} %constant_dynamic-slice_fusion.3), channel_id=1, source_target_pairs={{0,1},{1,0},{2,3},{3,2},{4,5},{5,4},{6,7},{7,6},{8,9},{9,8},{10,11... | collective-permute-start | bytes 6291464 | tf_op jit(solution)/shard_map/ppermute | solution.py:545
  622.9 19.8 %copy-start.30 = (f32[1,2048,256]{1,2,0:T(8,128)S(1)}, f32[1,2048,256]{1,2,0:T(8,128)}, u32[]{:S(2)}) copy-start(f32[1,2048,256]{1,2,0:T(8,128)} %get-tuple-element.151) | copy-start | bytes 6291460
  622.9 19.8 %copy-start.31 = (f32[1,2048,256]{1,2,0:T(8,128)S(1)}, f32[1,2048,256]{1,2,0:T(8,128)}, u32[]{:S(2)}) copy-start(f32[1,2048,256]{1,2,0:T(8,128)} %get-tuple-element.152) | copy-start | bytes 6291460
  638.4 54.2 %collective-permute-start.6 = (bf16[1024,1024]{1,0:T(8,128)(2,1)}, bf16[1024,1024]{1,0:T(8,128)(2,1)}, u32[]{:S(2)}, u32[]{:S(2)}) collective-permute-start(bf16[1024,1024]{1,0:T(8,128)(2,1)} %dynamic-slice_convert_fusion), channel_id=1, source_target_pairs={{0,1},{1,0},{2,3},{3,2},{4,5},{5,4},{6,7},{7,6},{8,9},{9,8},{10,11... | collective-permute-start | bytes 6291464 | tf_op jit(solution)/shard_map/ppermute | solution.py:564
  649.6 41.9 %collective-permute-start.7 = (bf16[1024,128]{1,0:T(8,128)(2,1)}, bf16[1024,128]{1,0:T(8,128)(2,1)S(1)}, u32[]{:S(2)}, u32[]{:S(2)}) collective-permute-start(bf16[1024,128]{1,0:T(8,128)(2,1)} %dynamic-slice_convert_fusion.4), channel_id=1, source_target_pairs={{0,1},{1,0},{2,3},{3,2},{4,5},{5,4},{6,7},{7,6},{8,9},{9,8},{10,11... | collective-permute-start | bytes 786440 | tf_op jit(solution)/shard_map/ppermute | solution.py:564
  651.9 38.4 %collective-permute-start.8 = (bf16[1024,16]{1,0:T(8,128)(2,1)}, bf16[1024,16]{1,0:T(8,128)(2,1)}, u32[]{:S(2)}, u32[]{:S(2)}) collective-permute-start(bf16[1024,16]{1,0:T(8,128)(2,1)} %dynamic-slice_convert_fusion.3), channel_id=1, source_target_pairs={{0,1},{1,0},{2,3},{3,2},{4,5},{5,4},{6,7},{7,6},{8,9},{9,8},{10,11... | collective-permute-start | bytes 98312 | tf_op jit(solution)/shard_map/ppermute | solution.py:564
  731.7 78.7 %collective-permute-start.5 = (bf16[2048,512]{1,0:T(8,128)(2,1)}, bf16[2048,512]{1,0:T(8,128)(2,1)}, u32[]{:S(2)}, u32[]{:S(2)}) collective-permute-start(bf16[2048,512]{1,0:T(8,128)(2,1)} %constant_dynamic-slice_fusion.1), channel_id=1, source_target_pairs={{0,1},{1,0},{2,3},{3,2},{4,5},{5,4},{6,7},{7,6},{8,9},{9,8},{10,11... | collective-permute-start | bytes 6291464 | tf_op jit(solution)/shard_map/ppermute | solution.py:545
  736.7 73.0 %copy-start.40 = (f32[64,2048]{1,0:T(8,128)S(1)}, f32[64,2048]{1,0:T(8,128)}, u32[]{:S(2)}) copy-start(f32[64,2048]{1,0:T(8,128)} %reduce-scatter.3.cloned.1.call-done) | copy-start | bytes 1572868
  (40 other events, 315.5 us)
Sparse Core Ops, SparseCore 0:
  44.1 55.8 all-gather.6
  102.7 49.0 all-gather.8
  154.1 49.2 all-gather.10
  428.1 105.8 reduce-scatter.2
  699.1 80.0 reduce-scatter.4
